TPU v7x, 256 devices: a whole 4x4x8 slice. The times are simulated.
256 devices in a mesh: gx: 64 (over x, z, core), gy: 4 (over y).
Axes of the slice: x: 4, y: 4, z: 8, core: 2. Of those that a mesh axis runs over, the one named last changes fastest.
Arguments:
- populations: float32 [19, 128, 40, 512], P(None, 'gx', None, 'gy'), may hold values from 0.5 to 1.5
- mass: float32 [128, 40, 512], P('gx', None, 'gy'), may hold values from 0.05 to 1
- cell_type: int32 [128, 40, 512], P('gx', None, 'gy'), may hold values from 0 to 2, as said below
- bubble_id: int32 [128, 40, 512], P('gx', None, 'gy'), may hold values from 0 to 63, as said below
- slab_source: int32 [64], replicated, may hold values from 0 to 63, each once
- gas_density: float32 [64], replicated, may hold values from 0.8 to 1.2
Outputs:
- distributions: float32 [19, 128, 40, 512], P(None, 'gx', None, 'gy')
- fluid_mass: float32 [128, 40, 512], P('gx', None, 'gy')
- gas_fraction: float32 [64], replicated
Inputs may be any that keep to these rules, and one draw needn't show every extreme that they name: `slab_source`: a permutation. `cell_type`: 0 gas, 1 interface, 2 liquid; the gas cells form 64 connected ellipsoidal blobs, and a gas cell's 18 lattice neighbours are gas or interface, never liquid. `bubble_id`: constant on the gas cells of one blob; every bubble has gas cells.
All inputs are finite; a program needn't handle non-finite values.
Results may differ from a plain program's by a relative error of at most 0.0003.
Values sent between devices are 32-bit elements; how exact they have to be, the bound alone decides.
A program may use at most 64 MiB of HBM per device.

v0:
```python
import jax
import jax.numpy as jnp
from jax import lax
from jax.sharding import PartitionSpec as P

BUBBLES = 64
ITERS = 3


LATTICE = (
    (0, 0, 0),
    (1, 0, 0),
    (-1, 0, 0),
    (0, 1, 0),
    (0, -1, 0),
    (0, 0, 1),
    (0, 0, -1),
    (1, 1, 0),
    (-1, -1, 0),
    (1, -1, 0),
    (-1, 1, 0),
    (1, 0, 1),
    (-1, 0, -1),
    (1, 0, -1),
    (-1, 0, 1),
    (0, 1, 1),
    (0, -1, -1),
    (0, 1, -1),
    (0, -1, 1),
)
OPPOSITE = (0, 2, 1, 4, 3, 6, 5, 8, 7, 10, 9, 12, 11, 14, 13, 16, 15, 18, 17)
WEIGHTS = (1.0 / 3.0,) + (1.0 / 18.0,) * 6 + (1.0 / 36.0,) * 12
OMEGA = 1.6


def with_halo(cells, sides, width):
    for axis, dim in sides:
        count = lax.axis_size(axis)
        head = lax.slice_in_dim(cells, 0, width, axis=dim)
        tail = lax.slice_in_dim(cells, cells.shape[dim] - width, cells.shape[dim], axis=dim)
        cells = jnp.concatenate(
            [
                lax.ppermute(tail, axis, [(i, (i + 1) % count) for i in range(count)]),
                cells,
                lax.ppermute(head, axis, [((i + 1) % count, i) for i in range(count)]),
            ],
            axis=dim,
        )
    return cells


def equilibrium(rho, speed_x, speed_y, speed_z):
    usq = speed_x * speed_x + speed_y * speed_y + speed_z * speed_z
    terms = []
    for index in range(19):
        step_x, step_y, step_z = LATTICE[index]
        along = step_x * speed_x + step_y * speed_y + step_z * speed_z
        terms.append(WEIGHTS[index] * rho * (1.0 + 3.0 * along + 4.5 * along * along - 1.5 * usq))
    return jnp.stack(terms)


def moments(dist):
    rho = jnp.sum(dist, axis=0)
    speeds = []
    for axis_pos in range(3):
        column = jnp.array([entry[axis_pos] for entry in LATTICE], jnp.float32)
        speeds.append(
            jnp.einsum("q,q...->...", column, dist, precision=lax.Precision.HIGHEST) / rho
        )
    return (rho, speeds)


def per_device(populations, mass, cell_type, bubble_id, slab_source, gas_density):
    slabs = lax.axis_size("gx")
    width = populations.shape[1]
    depth = populations.shape[2]
    across = populations.shape[3]
    payload = jnp.concatenate(
        [
            populations,
            mass[None],
            cell_type[None].astype(jnp.float32),
            bubble_id[None].astype(jnp.float32),
        ],
        axis=0,
    )
    spread = lax.all_to_all(
        payload.reshape(22, width, depth * across), "gx", split_axis=2, concat_axis=1, tiled=True
    )
    pieces = spread.reshape(22, slabs, width, -1)
    pieces = jnp.take(pieces, slab_source, axis=1).reshape(22, slabs * width, -1)
    home = lax.all_to_all(pieces, "gx", split_axis=1, concat_axis=2, tiled=True).reshape(
        22, width, depth, across
    )
    weight_col = jnp.array(WEIGHTS, jnp.float32).reshape(19, 1, 1, 1)
    dist = home[:19] * weight_col
    liquid_mass = home[19]
    kind = home[20].astype(jnp.int32)
    bubble = home[21].astype(jnp.int32)
    gas = kind == 0
    face = kind == 1
    liquid = kind == 2
    fluid = kind >= 1
    labels = jnp.arange(BUBBLES, dtype=jnp.int32)
    member = (bubble.reshape(1, -1) == labels[:, None]).astype(jnp.float32)

    def volumes(fill):
        share = jnp.where(gas, 1.0, jnp.where(face, 1.0 - fill, 0.0))
        part = jnp.dot(member, share.reshape(-1), precision=lax.Precision.HIGHEST)
        return lax.psum(part, ("gx", "gy"))

    def per_cell(table):
        return jnp.dot(table, member, precision=lax.Precision.HIGHEST).reshape(width, depth, across)

    row_index = lax.axis_index("gy")
    last_row = lax.axis_size("gy") - 1
    columns = jnp.arange(across + 2)
    outside = (columns == 0) & (row_index == 0) | (columns == across + 1) & (row_index == last_row)
    kind_ext = with_halo(kind, (("gx", 0), ("gy", 2)), 1)
    kind_ext = jnp.where(outside[None, None, :], -1, kind_ext)
    kind_fixed = jnp.pad(kind_ext, ((0, 0), (1, 1), (0, 0)), constant_values=-1)
    rho = jnp.sum(dist, axis=0)
    fill = jnp.where(liquid, 1.0, jnp.where(face, liquid_mass / rho, 0.0))
    start = volumes(fill)
    density = gas_density
    volume = start
    for step in range(ITERS):
        rho, speeds = moments(dist)
        speed_x, speed_y, speed_z = speeds
        post = jnp.where(
            fluid[None], dist - OMEGA * (dist - equilibrium(rho, speed_x, speed_y, speed_z)), dist
        )
        gas_rho = per_cell(density)
        gas_eq = equilibrium(gas_rho, speed_x, speed_y, speed_z)
        load = jnp.concatenate([post, fill[None]], axis=0)
        extended = with_halo(load, (("gx", 1), ("gy", 3)), 1)
        extended = jnp.pad(extended, ((0, 0), (0, 0), (1, 1), (0, 0)))
        post_pad = extended[:19]
        fill_pad = extended[19]
        incoming = []
        gained = jnp.zeros_like(rho)
        for index in range(19):
            step_x, step_y, step_z = LATTICE[index]
            back = OPPOSITE[index]
            window = (
                slice(1 - step_x, 1 - step_x + width),
                slice(1 - step_z, 1 - step_z + depth),
                slice(1 - step_y, 1 - step_y + across),
            )
            source = post_pad[index][window]
            near = kind_fixed[window]
            near_fill = fill_pad[window]
            rebuilt = gas_eq[index] + gas_eq[back] - post[back]
            incoming.append(jnp.where(near >= 1, source, jnp.where(near == 0, rebuilt, post[back])))
            share = jnp.where(near == 2, 1.0, jnp.where(near == 1, 0.5 * (fill + near_fill), 0.0))
            gained = gained + share * (source - post[back])
        read = jnp.stack(incoming)
        new_rho = jnp.sum(read, axis=0)
        liquid_mass = jnp.where(face, liquid_mass + gained, jnp.where(liquid, new_rho, 0.0))
        fill = jnp.where(liquid, 1.0, jnp.where(face, liquid_mass / new_rho, 0.0))
        volume = volumes(fill)
        density = gas_density * start / volume
        dist = jnp.where(gas[None], weight_col * per_cell(density)[None], read)
    total_cells = width * slabs * depth * across * lax.axis_size("gy")
    return (dist / weight_col, liquid_mass, volume * (BUBBLES / total_cells))


def solution(mesh):
    return jax.shard_map(
        per_device,
        mesh=mesh,
        in_specs=(
            P(None, "gx", None, "gy"),
            P("gx", None, "gy"),
            P("gx", None, "gy"),
            P("gx", None, "gy"),
            P(),
            P(),
        ),
        out_specs=(P(None, "gx", None, "gy"), P("gx", None, "gy"), P()),
        check_vma=False,
    )
```

profile of v0, /device:TPU:1, one launch (start us, length us, event | category | flops | bytes accessed | tf_op | source)
XLA Modules:
  0.0 557.5 jit_solution(3314679878358374630)
XLA Ops:
  5.0 4.9 copy.132
  9.9 9.7 %reshape.304 = f32[64,1,3520]{2,1,0:T(1,128)} reshape(f32[5120,2,22]{2,1,0:T(2,128)} %bitcast.941) | data formatting | bytes 1802240
  19.6 13.6 %all-to-all-start = ((f32[64,1,3520]{2,1,0:T(1,128)}), f32[64,1,3520]{2,1,0:T(1,128)S(1)}, u32[]{:S(2)}, u32[]{:S(2)}) async-start(f32[64,1,3520]{2,1,0:T(1,128)} %reshape.304), calls=%async_computation | async-start | bytes 1835008 | tf_op jit(solution)/shard_map/all_to_all | solution.py:87
  33.4 25.3 %all-to-all-done = f32[64,1,3520]{2,1,0:T(1,128)S(1)} async-done(((f32[64,1,3520]{2,1,0:T(1,128)}), f32[64,1,3520]{2,1,0:T(1,128)S(1)}, u32[]{:S(2)}, u32[]{:S(2)}) %all-to-all-start) | async-done | bytes 901152 | tf_op jit(solution)/shard_map/all_to_all | solution.py:87
  59.3 2.8 reduce.58
  62.1 10.4 %reshape.305 = f32[5120,2,22]{2,1,0:T(2,128)} reshape(f32[64,3520]{1,0:T(8,128)S(1)} %reduce.58) | data formatting | bytes 1802240
  72.5 7.1 %copy.134 = f32[22,2,64,80]{3,1,2,0:T(2,128)S(1)} copy(f32[22,2,64,80]{0,1,3,2:T(2,128)} %bitcast.942) | data formatting | bytes 1802240 | tf_op jit(solution)/shard_map/all_to_all | solution.py:87
  79.7 2.7 gather_fusion
  85.5 6.5 %all-to-all-start.1 = ((f32[22,128,80]{2,0,1:T(8,128)}), f32[22,128,80]{2,0,1:T(8,128)S(1)}, u32[]{:S(2)}, u32[]{:S(2)}) async-start(f32[22,128,80]{2,0,1:T(8,128)} %copy.136), calls=%async_computation.1 | async-start | bytes 3145728 | tf_op jit(solution)/shard_map/all_to_all | solution.py:92
  92.5 39.1 %all-to-all-done.1 = f32[22,128,80]{2,0,1:T(8,128)S(1)} async-done(((f32[22,128,80]{2,0,1:T(8,128)}), f32[22,128,80]{2,0,1:T(8,128)S(1)}, u32[]{:S(2)}, u32[]{:S(2)}) %all-to-all-start.1) | async-done | bytes 901152 | tf_op jit(solution)/shard_map/all_to_all | solution.py:92
  169.9 2.7 copy.143
  175.8 4.3 collective-permute-done.6
  184.1 4.3 select_maximum_fusion.10
  196.5 80.7 %all-reduce.4 = (f32[64]{0:T(128)S(1)}, f32[64]{0:T(128)S(1)}) all-reduce(f32[64]{0:T(128)S(1)} %copy-done.134, f32[64]{0:T(128)S(1)} %fusion.18), channel_id=1, replica_groups=mesh['gx'=64,'gy'=4] {'gx','gy'}, use_global_device_ids=true, to_apply=%region_1.2 | all-reduce | flops 128 | bytes 1024 | tf_op jit(solution)/shard_map/psum | solution.py:110
  302.9 4.4 collective-permute-done.8
  307.3 2.8 collective-permute-done.9
  322.4 4.3 select_maximum_fusion.5
  328.1 3.1 fusion.503
  333.3 80.9 %psum.30 = f32[64]{0:T(128)S(1)} all-reduce(f32[64]{0:T(128)S(1)} %fusion.19), channel_id=1, replica_groups=mesh['gx'=64,'gy'=4] {'gx','gy'}, use_global_device_ids=true, to_apply=%region_4.5 | all-reduce | flops 64 | bytes 512 | tf_op jit(solution)/shard_map/psum | solution.py:110
  443.0 4.3 collective-permute-done.12
  447.3 3.0 collective-permute-done.13
  456.1 2.7 collective-permute-start.15
  463.3 4.3 select_maximum_fusion
  474.0 80.5 %psum.31 = f32[64]{0:T(128)S(1)} all-reduce(f32[64]{0:T(128)S(1)} %fusion.20), channel_id=1, replica_groups=mesh['gx'=64,'gy'=4] {'gx','gy'}, use_global_device_ids=true, to_apply=%region_6.7 | all-reduce | flops 64 | bytes 512 | tf_op jit(solution)/shard_map/psum | solution.py:110
  (515 shorter events, 150.0 us)
Async XLA Ops:
  19.6 39.2 %all-to-all-start = ((f32[64,1,3520]{2,1,0:T(1,128)}), f32[64,1,3520]{2,1,0:T(1,128)S(1)}, u32[]{:S(2)}, u32[]{:S(2)}) async-start(f32[64,1,3520]{2,1,0:T(1,128)} %reshape.304), calls=%async_computation | async-start | bytes 1835008 | tf_op jit(solution)/shard_map/all_to_all | solution.py:87
  85.5 46.2 %all-to-all-start.1 = ((f32[22,128,80]{2,0,1:T(8,128)}), f32[22,128,80]{2,0,1:T(8,128)S(1)}, u32[]{:S(2)}, u32[]{:S(2)}) async-start(f32[22,128,80]{2,0,1:T(8,128)} %copy.136), calls=%async_computation.1 | async-start | bytes 3145728 | tf_op jit(solution)/shard_map/all_to_all | solution.py:92
  139.6 22.4 %collective-permute-start = (s32[1,40,128]{2,1,0:T(8,128)}, s32[1,40,128]{2,1,0:T(8,128)S(1)}, u32[]{:S(2)}, u32[]{:S(2)}) collective-permute-start(s32[1,40,128]{2,1,0:T(8,128)} %slice.1048), channel_id=1, source_target_pairs={{0,4},{4,8},{8,12},{12,16},{16,20},{20,24},{24,28},{28,32},{32,36}... | collective-permute-start | bytes 61448 | tf_op jit(solution)/shard_map/ppermute | solution.py:43
  140.5 21.5 %collective-permute-start.1 = (s32[1,40,128]{2,1,0:T(8,128)S(1)}, s32[1,40,128]{2,1,0:T(8,128)S(1)}, u32[]{:S(2)}, u32[]{:S(2)}) collective-permute-start(s32[1,40,128]{2,1,0:T(8,128)S(1)} %slice.1050), channel_id=1, source_target_pairs={{4,0},{8,4},{12,8},{16,12},{20,16},{24,20},{28,24},{32,28},{36,32}... | collective-permute-start | bytes 61448 | tf_op jit(solution)/shard_map/ppermute | solution.py:45
  157.5 10.5 %collective-permute-start.4 = (f32[20,1,40,128]{3,2,1,0:T(8,128)S(1)}, f32[20,1,40,128]{3,2,1,0:T(8,128)S(1)}, u32[]{:S(2)}, u32[]{:S(2)}) collective-permute-start(f32[20,1,40,128]{3,2,1,0:T(8,128)S(1)} %get-tuple-element.359), channel_id=1, source_target_pairs={{0,4},{4,8},{8,12},{12,16},{16,20},{20,24},{24,28},{28,32},{32,36}... | collective-permute-start | bytes 1228808 | tf_op jit(solution)/shard_map/ppermute | solution.py:43
  159.3 8.7 %collective-permute-start.5 = (f32[20,1,40,128]{3,2,1,0:T(8,128)S(1)}, f32[20,1,40,128]{3,2,1,0:T(8,128)S(1)}, u32[]{:S(2)}, u32[]{:S(2)}) collective-permute-start(f32[20,1,40,128]{3,2,1,0:T(8,128)S(1)} %get-tuple-element.360), channel_id=1, source_target_pairs={{4,0},{8,4},{12,8},{16,12},{20,16},{24,20},{28,24},{32,28},{36,32}... | collective-permute-start | bytes 1228808 | tf_op jit(solution)/shard_map/ppermute | solution.py:45
  162.1 5.7 %collective-permute-start.2 = (s32[4,40,1]{2,1,0:T(8,128)S(1)}, s32[4,40,1]{2,1,0:T(8,128)S(1)}, u32[]{:S(2)}, u32[]{:S(2)}) collective-permute-start(s32[4,40,1]{2,1,0:T(8,128)S(1)} %get-tuple-element.363), channel_id=1, source_target_pairs={{0,1},{1,2},{2,3},{3,0},{4,5},{5,6},{6,7},{7,4},{8,9},{9,10},{10,1... | collective-permute-start | bytes 1928 | tf_op jit(solution)/shard_map/ppermute | solution.py:43
  163.5 4.3 collective-permute-start.3
  173.8 7.7 %collective-permute-start.7 = (f32[20,4,40,1]{2,1,3,0:T(4,128)}, f32[20,4,40,1]{2,1,3,0:T(4,128)}, u32[]{:S(2)}, u32[]{:S(2)}) collective-permute-start(f32[20,4,40,1]{2,1,3,0:T(4,128)} %copy.144), channel_id=1, source_target_pairs={{1,0},{2,1},{3,2},{0,3},{5,4},{6,5},{7,6},{4,7},{9,8},{10,9},{11,1... | collective-permute-start | bytes 38408 | tf_op jit(solution)/shard_map/ppermute | solution.py:45
  175.7 4.4 collective-permute-start.6
  195.2 92.7 %copy-start.126 = (f32[19,1,1,1]{0,1,3,2:T(1,128)S(1)}, f32[19,1,1,1]{0,1,3,2:T(1,128)}, u32[]{:S(2)}) copy-start(f32[19,1,1,1]{0,1,3,2:T(1,128)} %constant.85) | copy-start | bytes 232
  302.1 5.2 collective-permute-start.8
  302.4 7.7 %collective-permute-start.9 = (f32[20,1,40,128]{3,2,1,0:T(8,128)S(1)}, f32[20,1,40,128]{3,2,1,0:T(8,128)S(1)}, u32[]{:S(2)}, u32[]{:S(2)}) collective-permute-start(f32[20,1,40,128]{3,2,1,0:T(8,128)S(1)} %get-tuple-element.358), channel_id=1, source_target_pairs={{4,0},{8,4},{12,8},{16,12},{20,16},{24,20},{28,24},{32,28},{36,32}... | collective-permute-start | bytes 1228808 | tf_op jit(solution)/shard_map/ppermute | solution.py:45
  314.0 4.1 collective-permute-start.10
  316.5 3.3 collective-permute-start.11
  331.2 95.7 %copy-start.68 = (f32[2,40,128]{2,1,0:T(8,128)S(1)}, f32[2,40,128]{2,1,0:T(8,128)}, u32[]{:S(2)}) copy-start(f32[2,40,128]{2,1,0:T(8,128)} %get-tuple-element.34) | copy-start | bytes 122884
  331.2 95.7 %copy-start.67 = (f32[2,40,128]{2,1,0:T(8,128)S(1)}, f32[2,40,128]{2,1,0:T(8,128)}, u32[]{:S(2)}) copy-start(f32[2,40,128]{2,1,0:T(8,128)} %get-tuple-element.33) | copy-start | bytes 122884
  331.2 95.7 %copy-start.66 = (f32[2,40,128]{2,1,0:T(8,128)S(1)}, f32[2,40,128]{2,1,0:T(8,128)}, u32[]{:S(2)}) copy-start(f32[2,40,128]{2,1,0:T(8,128)} %get-tuple-element.32) | copy-start | bytes 122884
  331.2 95.7 %copy-start.65 = (f32[2,40,128]{2,1,0:T(8,128)S(1)}, f32[2,40,128]{2,1,0:T(8,128)}, u32[]{:S(2)}) copy-start(f32[2,40,128]{2,1,0:T(8,128)} %get-tuple-element.31) | copy-start | bytes 122884
  331.2 95.7 %copy-start.64 = (f32[2,40,128]{2,1,0:T(8,128)S(1)}, f32[2,40,128]{2,1,0:T(8,128)}, u32[]{:S(2)}) copy-start(f32[2,40,128]{2,1,0:T(8,128)} %get-tuple-element.30) | copy-start | bytes 122884
  441.6 5.7 %collective-permute-start.12 = (f32[20,1,40,128]{3,2,1,0:T(8,128)S(1)}, f32[20,1,40,128]{3,2,1,0:T(8,128)S(1)}, u32[]{:S(2)}, u32[]{:S(2)}) collective-permute-start(f32[20,1,40,128]{3,2,1,0:T(8,128)S(1)} %get-tuple-element.355), channel_id=1, source_target_pairs={{0,4},{4,8},{8,12},{12,16},{16,20},{20,24},{24,28},{28,32},{32,36}... | collective-permute-start | bytes 1228808 | tf_op jit(solution)/shard_map/ppermute | solution.py:43
  442.4 7.9 %collective-permute-start.13 = (f32[20,1,40,128]{3,2,1,0:T(8,128)S(1)}, f32[20,1,40,128]{3,2,1,0:T(8,128)S(1)}, u32[]{:S(2)}, u32[]{:S(2)}) collective-permute-start(f32[20,1,40,128]{3,2,1,0:T(8,128)S(1)} %get-tuple-element.356), channel_id=1, source_target_pairs={{4,0},{8,4},{12,8},{16,12},{20,16},{24,20},{28,24},{32,28},{36,32}... | collective-permute-start | bytes 1228808 | tf_op jit(solution)/shard_map/ppermute | solution.py:45
  454.9 4.4 collective-permute-start.14
  456.1 4.5 collective-permute-start.15
  (129 other events, 763.0 us)
where the time goes:
time: 566 us; the launch traced here: 557 us
  blocking collectives  242 us (43%)
  local copies, waits for them, and re-layouts  97.1 us (17%)
  waiting for transfers between devices  84.7 us (15%)
  other arithmetic  72.1 us (13%)
  starting transfers between devices  38.3 us (7%)
  matrix products  19.9 us (4%)
    psum x3, blocking collectives, volumes(): return lax.psum(part, ('gx', 'gy'))  242 us
    unnamed x323, local copies, waits for them, and re-layouts  40.4 us
    all_to_all x1, waiting for transfers between devices, per_device(): lax.all_to_all(pieces, 'gx', split_axis=1, concat_axis=2, tiled=True)  39.1 us
    unnamed x59, other arithmetic  37.3 us
    all_to_all x1, waiting for transfers between devices, per_device(): lax.all_to_all(payload.reshape(22, width, depth * across), 'gx', split_ax...  25.3 us
    all_to_all x1, starting transfers between devices, per_device(): lax.all_to_all(payload.reshape(22, width, depth * across), 'gx', split_ax...  13.6 us
    ppermute x8, waiting for transfers between devices, with_halo(): lax.ppermute(tail, axis, [(i, (i + 1) % count) for i in range(count)])  13.5 us
    slice x8, local copies, waits for them, and re-layouts, with_halo(): lax.slice_in_dim(cells, cells.shape[dim] - width, cells.shape[dim], axis=...  13.4 us
  transfers between devices with their start and end apart: 18, of which 9 were waited for; matrix products, arithmetic and copies ran while one was open for 5% of the time, Pallas kernels for 0%

commit v1 on v0

v1 whole, which is shorter than its diff:
```python
import functools

import jax
import jax.numpy as jnp
from jax import lax
from jax.experimental import pallas as pl
from jax.experimental.pallas import tpu as pltpu
from jax.sharding import PartitionSpec as P

BUBBLES = 64
ITERS = 3
OMEGA = 1.6
MESH = pl.DeviceIdType.MESH
F32 = jnp.float32

LATTICE = (
    (0, 0, 0),
    (1, 0, 0),
    (-1, 0, 0),
    (0, 1, 0),
    (0, -1, 0),
    (0, 0, 1),
    (0, 0, -1),
    (1, 1, 0),
    (-1, -1, 0),
    (1, -1, 0),
    (-1, 1, 0),
    (1, 0, 1),
    (-1, 0, -1),
    (1, 0, -1),
    (-1, 0, 1),
    (0, 1, 1),
    (0, -1, -1),
    (0, 1, -1),
    (0, -1, 1),
)
HALF = 19
ORDER = (1, 7, 9, 11, 13, HALF, 2, 8, 10, 12, 14, 0, 3, 4, 5, 6, 15, 16, 17, 18)
AT = {field: pos for pos, field in enumerate(ORDER)}
KIND = 20
COLS_UP = (3, 7, 10, 15, 17, HALF, KIND)
COLS_DOWN = (4, 8, 9, 16, 18, HALF, KIND)
PAIRS = ((1, 2), (3, 4), (5, 6), (7, 8), (9, 10), (11, 12), (13, 14), (15, 16), (17, 18))
PAD = 8


def pair_speeds(ux, uy, uz):
    return (ux, uy, uz, ux + uy, ux - uy, ux + uz, ux - uz, uy + uz, uy - uz)


def kernel(
    shape,
    pop,
    mass,
    cell,
    label,
    source,
    gas_density,
    out_g,
    out_m,
    out_v,
    stage,
    got,
    sorted_pieces,
    home,
    post,
    kinds,
    near,
    waiting,
    speed,
    bubble,
    reversed_label,
    fluid_mass,
    share,
    base_rho,
    gas_rho,
    gain,
    gas_here,
    members,
    cols_out,
    cols_in,
    cols,
    sums_a,
    sums_b,
    part,
    send,
    recv,
):
    nx, nz, ny = shape
    ngx = nx * nz * 2
    chips = nx * nz
    per = tiles_per_chip(chips)
    big = (per + 1) // 2
    small = per - big
    gx = lax.axis_index("gx")
    gy = lax.axis_index("gy")
    core = gx % 2
    chip = gx // 2
    pos_x = chip // nz
    pos_z = chip % nz
    right = (gx + 1) % ngx
    left = (gx + ngx - 1) % ngx
    lane = lax.broadcasted_iota(jnp.int32, (8, 128), 1)

    SPREAD, GATHER, KINDS = 0, 1, 2

    def x_sem(step, side):
        return 4 + step * 8 + side

    def y_sem(step, side):
        return 4 + step * 8 + 2 + side

    def a_sem(step):
        return 4 + step * 8 + 4

    def b_sem(step):
        return 4 + step * 8 + 5

    def remote(src, dst, sem, to_x, to_y):
        return pltpu.make_async_remote_copy(
            src_ref=src,
            dst_ref=dst,
            send_sem=send.at[sem],
            recv_sem=recv.at[sem],
            device_id=(to_x, to_y),
            device_id_type=MESH,
        )

    def wait_bytes(ref, sem):
        pltpu.make_async_copy(ref, ref, sem).wait()

    barrier = pltpu.get_barrier_semaphore()

    def greet_x(k, carry):
        pl.semaphore_signal(
            barrier, inc=1, device_id=((gx + k) % ngx, gy), device_id_type=MESH
        )
        return carry

    lax.fori_loop(1, ngx, greet_x, 0)
    group_a = nz * 2
    group_b = nx * ny
    at_a = gx % group_a
    at_b = pos_x * ny + gy

    def peer_b(k):
        other = (at_b + k) % group_b
        return (other // ny) * group_a + at_a, other % ny

    greeted = ngx - 1

    def greet_b(k, carry):
        to_x, to_y = peer_b(k)

        @pl.when(to_y != gy)
        def _():
            pl.semaphore_signal(barrier, inc=1, device_id=(to_x, to_y), device_id_type=MESH)

        return carry

    lax.fori_loop(1, group_b, greet_b, 0)
    greeted += group_b - nx
    for to_x in (left, right):
        for to_y in ((gy + 1) % ny, (gy + ny - 1) % ny):
            pl.semaphore_signal(barrier, inc=1, device_id=(to_x, to_y), device_id_type=MESH)
    greeted += 4

    stage[0:190] = pop[...]
    stage[190:200] = mass[...]
    stage[200:210] = cell[...].astype(F32)
    stage[210:220] = label[...].astype(F32)
    walls = jnp.full((PAD, 128), -1.0, F32)
    for slot in range(4):
        kinds[slot, 0:PAD] = walls
        kinds[slot, PAD + 40 : PAD + 48] = walls
    for side in range(2):
        cols[side, 0:PAD] = walls
        cols[side, PAD + 40 : PAD + 48] = walls
    pl.semaphore_wait(barrier, greeted)

    def peer_chip(k):
        dz = (3 * (k // nx) + nz // 2) % nz
        dx = k % nx
        return ((pos_x + dx) % nx) * nz + (pos_z + dz) % nz

    def spread(k, carry):
        to = peer_chip(k)
        for side, tiles in ((0, big), (1, small)):
            peer = to * 2 + side

            @pl.when(peer != gx)
            def _():
                remote(
                    stage.at[pl.ds(to * per + side * big, tiles)],
                    got.at[gx, pl.ds(0, tiles)],
                    SPREAD,
                    peer,
                    gy,
                ).start()

        return carry

    lax.fori_loop(0, chips, spread, 0)
    mine = chip * per + core * big
    got[gx] = stage[pl.ds(mine, big)]

    def take(k, carry):
        sorted_pieces[k] = got[source[k]]
        return carry

    for side, tiles in ((0, big), (1, small)):

        @pl.when(core == side)
        def _():
            wait_bytes(got.at[pl.ds(0, ngx - 1), pl.ds(0, tiles)], recv.at[SPREAD])

    lax.fori_loop(0, ngx, take, 0, unroll=4)

    def gather(k, carry):
        to = peer_chip(k)
        for other in range(2):
            peer = to * 2 + other
            for side, tiles in ((0, big), (1, small)):

                @pl.when((peer != gx) & (core == side))
                def _():
                    remote(
                        sorted_pieces.at[peer, pl.ds(0, tiles)],
                        home.at[pl.ds(chip * per + side * big, tiles)],
                        GATHER,
                        peer,
                        gy,
                    ).start()

        return carry

    lax.fori_loop(0, chips, gather, 0)
    for side, tiles in ((0, big), (1, small)):

        @pl.when(core == side)
        def _():
            home[pl.ds(chip * per + side * big, tiles)] = sorted_pieces[gx, 0:tiles]
            wait_bytes(home.at[pl.ds(0, chips * per - tiles)], recv.at[GATHER])

    for x in range(2):
        for z in range(5):
            kinds[x + 1, PAD + z * 8 : PAD + z * 8 + 8] = home[200 + x * 5 + z]
    rows = pl.ds(PAD, 40)
    kinds_right = remote(kinds.at[2, rows], kinds.at[0, rows], KINDS, right, gy)
    kinds_left = remote(kinds.at[1, rows], kinds.at[3, rows], KINDS + 1, left, gy)
    kinds_right.start()
    kinds_left.start()

    def collide(step, i, g):
        x, z = i // 5, i % 5
        diff = [g[a] - g[b] for a, b in PAIRS]
        total = [g[a] + g[b] for a, b in PAIRS]
        faces = total[0] + total[1] + total[2]
        edges = (total[3] + total[4]) + (total[5] + total[6]) + (total[7] + total[8])
        rho = g[0] * (1.0 / 3.0) + faces * (1.0 / 18.0) + edges * (1.0 / 36.0)
        inv = 1.0 / rho
        ux = (diff[0] * (1.0 / 18.0) + (diff[3] + diff[4] + diff[5] + diff[6]) * (1.0 / 36.0)) * inv
        uy = (diff[1] * (1.0 / 18.0) + (diff[3] - diff[4] + diff[7] + diff[8]) * (1.0 / 36.0)) * inv
        uz = (diff[2] * (1.0 / 18.0) + (diff[5] - diff[6] + diff[7] - diff[8]) * (1.0 / 36.0)) * inv
        speed[0, i] = ux
        speed[1, i] = uy
        speed[2, i] = uz
        scaled = OMEGA * rho
        flat = scaled * (1.0 - 1.5 * (ux * ux + uy * uy + uz * uz))
        at = pl.ds(pl.multiple_of(PAD + z * 8, 8), 8)
        post[step, x + 1, AT[0], at] = flat + (1.0 - OMEGA) * g[0]
        square = 4.5 * scaled
        line = 3.0 * scaled
        for (a, b), along in zip(PAIRS, pair_speeds(ux, uy, uz)):
            even = flat + square * (along * along)
            odd = line * along
            post[step, x + 1, AT[a], at] = even + odd + (1.0 - OMEGA) * g[a]
            post[step, x + 1, AT[b], at] = even - odd + (1.0 - OMEGA) * g[b]
        return rho

    def put_half(step, i, value):
        x, z = i // 5, i % 5
        post[step, x + 1, AT[HALF], pl.ds(pl.multiple_of(PAD + z * 8, 8), 8)] = 0.5 * value

    def level(kind, liquid_mass, rho):
        phi = jnp.where(kind == 2.0, 1.0, jnp.where(kind == 1.0, liquid_mass / rho, 0.0))
        part_gas = jnp.where(kind == 0.0, 1.0, jnp.where(kind == 1.0, 1.0 - phi, 0.0))
        return phi, part_gas

    def send_faces(step):
        plus = remote(
            post.at[step, 2, pl.ds(0, 6), rows],
            post.at[step, 0, pl.ds(0, 6), rows],
            x_sem(step, 0),
            right,
            gy,
        )
        minus = remote(
            post.at[step, 1, pl.ds(5, 6), rows],
            post.at[step, 3, pl.ds(5, 6), rows],
            x_sem(step, 1),
            left,
            gy,
        )
        plus.start()
        minus.start()

        def pack(z, carry):
            at = pl.ds(pl.multiple_of(PAD + z * 8, 8), 8)
            up = jnp.zeros((8, 128), F32)
            down = jnp.zeros((8, 128), F32)
            for j in range(7 if step == 0 else 6):
                for x in range(2):
                    spot = j * 4 + x + 1
                    if COLS_UP[j] == KIND:
                        high = low = kinds[x + 1, at]
                    else:
                        high = post[step, x + 1, AT[COLS_UP[j]], at]
                        low = post[step, x + 1, AT[COLS_DOWN[j]], at]
                    up = jnp.where(lane == spot, pltpu.roll(high, spot + 1, 1), up)
                    down = jnp.where(lane == spot, pltpu.roll(low, spot, 1), down)
            to = pl.ds(pl.multiple_of(z * 8, 8), 8)
            cols_out[step, 0, to] = up
            cols_out[step, 1, to] = down
            return carry

        lax.fori_loop(0, 5, pack, 0)
        for side, there, to_y in ((0, gy < ny - 1, gy + 1), (1, gy > 0, gy - 1)):

            @pl.when(there)
            def _():
                for shift, to_x in ((-1, left), (0, gx), (1, right)):
                    remote(
                        cols_out.at[step, side],
                        cols_in.at[step, side, 1 - shift],
                        y_sem(step, side),
                        to_x,
                        to_y,
                    ).start()

        return plus, minus

    def wait_columns(step):
        for side, there in ((0, gy > 0), (1, gy < ny - 1)):

            @pl.when(there)
            def _():
                wait_bytes(cols_in.at[step, side], recv.at[y_sem(step, side)])

            def merge(z, carry):
                of = pl.ds(pl.multiple_of(z * 8, 8), 8)
                before = pltpu.roll(cols_in[step, side, 0, of], 126, 1)
                after = pltpu.roll(cols_in[step, side, 2, of], 2, 1)
                slot = lane % 4
                here = cols_in[step, side, 1, of]
                cols[side, pl.ds(pl.multiple_of(PAD + z * 8, 8), 8)] = jnp.where(
                    slot == 0, before, jnp.where(slot == 3, after, here)
                )
                return carry

            lax.fori_loop(0, 5, merge, 0)

    def shifted(value, step_y, j, slot, at, outside):
        if step_y == 0:
            return value
        if step_y == 1:
            edge = pltpu.roll(cols[0, at], 128 - (j * 4 + slot), 1)
            if outside is not None:
                edge = jnp.where(outside[0], -1.0, edge)
            return jnp.where(lane == 0, edge, pltpu.roll(value, 1, 1))
        edge = pltpu.roll(cols[1, at], 127 - (j * 4 + slot), 1)
        if outside is not None:
            edge = jnp.where(outside[1], -1.0, edge)
        return jnp.where(lane == 127, edge, pltpu.roll(value, 127, 1))

    def find_near(i, carry):
        x, z = i // 5, i % 5
        row = PAD + z * 8
        for d in range(1, 19):
            step_x, step_y, step_z = LATTICE[d]
            slot = x + 1 - step_x
            at = pl.ds(row - step_z, 8)
            near[d, i] = shifted(kinds[slot, at], step_y, 6, slot, at, (gy == 0, gy == ny - 1))
        return carry

    def twice_even(i):
        ux, uy, uz = speed[0, i], speed[1, i], speed[2, i]
        flat = 2.0 - 3.0 * (ux * ux + uy * uy + uz * uz)
        return [flat + 9.0 * (along * along) for along in pair_speeds(ux, uy, uz)]

    def stream(step, i):
        x, z = i // 5, i % 5
        row = PAD + z * 8
        own = pl.ds(pl.multiple_of(row, 8), 8)
        half = post[step, x + 1, AT[HALF], own]
        rest = post[step, x + 1, AT[0], own]
        waiting[0, i] = rest
        zero = jnp.zeros((8, 128), F32)
        rho_sum = [zero, zero]
        gas_sum = [zero, zero]
        gain_sum = [zero, zero]
        for k, ((a, b), even) in enumerate(zip(PAIRS, twice_even(i))):
            kind_of = 0 if k < 3 else 1
            here = {a: post[step, x + 1, AT[a], own], b: post[step, x + 1, AT[b], own]}
            for d, back in ((a, b), (b, a)):
                step_x, step_y, step_z = LATTICE[d]
                slot = x + 1 - step_x
                at = pl.ds(row - step_z, 8)
                j = 0 if step_y == 0 else (COLS_UP if step_y == 1 else COLS_DOWN).index(d)
                came = shifted(post[step, slot, AT[d], at], step_y, j, slot, at, None)
                near_half = shifted(post[step, slot, AT[HALF], at], step_y, 5, slot, at, None)
                kind = near[d, i]
                bounced = here[back]
                value = jnp.where(kind >= 1.0, came, bounced)
                gas = kind == 0.0
                known = jnp.where(gas, -bounced, value)
                waiting[d, i] = known
                rho_sum[kind_of] = rho_sum[kind_of] + known
                gas_sum[kind_of] = gas_sum[kind_of] + jnp.where(gas, even, 0.0)
                part_of = jnp.where(
                    kind == 2.0, 1.0, jnp.where(kind == 1.0, half + near_half, 0.0)
                )
                gain_sum[kind_of] = gain_sum[kind_of] + part_of * (value - bounced)
        base_rho[i] = (
            rest * (1.0 / 3.0) + rho_sum[0] * (1.0 / 18.0) + rho_sum[1] * (1.0 / 36.0)
        )
        gas_rho[i] = gas_sum[0] * (1.0 / 18.0) + gas_sum[1] * (1.0 / 36.0)
        gain[i] = gain_sum[0] * (1.0 / 18.0) + gain_sum[1] * (1.0 / 36.0)

    def arrived(i):
        density = gas_here[i]
        g = [waiting[0, i]] + [None] * 18
        for (a, b), even in zip(PAIRS, twice_even(i)):
            lift = density * even
            for d in (a, b):
                known = waiting[d, i]
                g[d] = jnp.where(near[d, i] == 0.0, known + lift, known)
        return g

    def lookup(table):
        def one(i, carry):
            gas_here[i] = jnp.take_along_axis(
                table, bubble[i], axis=1, mode="promise_in_bounds"
            )
            return carry

        lax.fori_loop(0, 10, one, 0, unroll=5)

    def member_sums():
        def one(b, carry):
            members[b] = jnp.sum(jnp.where(reversed_label[...] == b, share[...], 0.0), axis=0)
            return carry

        lax.fori_loop(0, BUBBLES, one, 0, unroll=8)
        now = members[...]
        for bit in range(6):
            half = now.shape[0] // 2
            first, second = now[:half], now[half:]
            odd = ((lax.broadcasted_iota(jnp.int32, first.shape, 2) >> bit) & 1) == 1
            keep = jnp.where(odd, second, first)
            move = jnp.where(odd, first, second)
            now = keep + pltpu.roll(move, 128 - (1 << bit), 2)
        now = now[0]
        return now + pltpu.roll(now, 64, 1)

    def send_sums(dst, own, sem, step, stage_no, count, peer_of):
        def one(k, carry):
            to_x, to_y = peer_of(k)
            remote(part.at[step, stage_no], dst.at[step, own], sem, to_x, to_y).start()
            return carry

        lax.fori_loop(1, count, one, 0)

    def peer_a(k):
        return gx - at_a + (at_a + k) % group_a, gy

    def begin_sum(step, value):
        part[step, 0] = value
        sums_a[step, at_a] = value
        send_sums(sums_a, at_a, a_sem(step), step, 0, group_a, peer_a)

    def middle_sum(step):
        wait_bytes(sums_a.at[step, pl.ds(0, group_a - 1)], recv.at[a_sem(step)])
        value = jnp.sum(sums_a[step], axis=0)
        part[step, 1] = value
        sums_b[step, at_b] = value
        send_sums(sums_b, at_b, b_sem(step), step, 1, group_b, peer_b)

    def end_sum(step):
        wait_bytes(sums_b.at[step, pl.ds(0, group_b - 1)], recv.at[b_sem(step)])
        value = jnp.sum(jnp.sum(sums_b[step], axis=0), axis=0, keepdims=True)
        return jnp.broadcast_to(value, (8, 128))

    def first(i, carry):
        rho = collide(0, i, [home[q * 10 + i] for q in range(19)])
        kind = home[200 + i]
        phi, part_gas = level(kind, home[190 + i], rho)
        put_half(0, i, phi)
        share[i] = part_gas
        fluid_mass[i] = home[190 + i]
        return carry

    lax.fori_loop(0, 10, first, 0)
    faces = send_faces(0)
    started = [faces]
    label_now = home[210:220].astype(jnp.int32)
    bubble[...] = label_now
    turned = jnp.zeros_like(label_now)
    for bit in range(6):
        turned = turned | (((label_now >> bit) & 1) << (5 - bit))
    reversed_label[...] = turned
    volume_start = member_sums()
    bubble_lane = lane & (BUBBLES - 1)
    table = jnp.zeros((8, 128), F32)
    for b in range(BUBBLES):
        table = jnp.where(bubble_lane == b, gas_density[b], table)
    density_start = table
    lookup(table)

    kinds_right.wait_recv()
    kinds_left.wait_recv()
    wait_columns(0)
    lax.fori_loop(0, 10, find_near, 0)
    for face in faces:
        face.wait_recv()

    def stream_all(step):
        def one(i, carry):
            stream(step, i)
            return carry

        lax.fori_loop(0, 10, one, 0)

    stream_all(0)
    start_total = None
    for step in range(ITERS):

        def settle(i, carry):
            kind = home[200 + i]
            rho = base_rho[i] + gas_here[i] * gas_rho[i]
            liquid_mass = jnp.where(
                kind == 1.0, fluid_mass[i] + gain[i], jnp.where(kind == 2.0, rho, 0.0)
            )
            fluid_mass[i] = liquid_mass
            phi, part_gas = level(kind, liquid_mass, rho)
            if step < ITERS - 1:
                put_half(step + 1, i, phi)
            share[i] = part_gas
            return carry

        lax.fori_loop(0, 10, settle, 0, unroll=5)
        volume = member_sums()
        if step == 0:
            volume = jnp.where(lane < BUBBLES, volume, volume_start)
        begin_sum(step, volume)

        if step < ITERS - 1:

            def again(i, carry):
                collide(step + 1, i, arrived(i))
                return carry

            lax.fori_loop(0, 10, again, 0)
            faces = send_faces(step + 1)
            started.append(faces)
            middle_sum(step)
            wait_columns(step + 1)
            for face in faces:
                face.wait_recv()
            stream_all(step + 1)
        else:

            def last(i, carry):
                for q, value in enumerate(arrived(i)):
                    out_g[q * 10 + i] = value
                return carry

            lax.fori_loop(0, 10, last, 0)
            middle_sum(step)
        total = end_sum(step)
        if step == 0:
            other = pltpu.roll(total, 64, 1)
            start_total = jnp.where(lane < BUBBLES, other, total)
            total = jnp.where(lane < BUBBLES, total, other)
        lookup(density_start * start_total / total)

    def finish(i, carry):
        gas = home[200 + i] == 0.0
        density = gas_here[i]
        for q in range(19):
            out_g[q * 10 + i] = jnp.where(gas, density, out_g[q * 10 + i])
        return carry

    lax.fori_loop(0, 10, finish, 0)
    out_m[...] = fluid_mass[...]
    out_v[...] = total * (BUBBLES / (ngx * ny * 2 * 40 * 128))

    for side, tiles in ((0, big), (1, small)):

        @pl.when(core == side)
        def _():
            wait_bytes(stage.at[pl.ds(0, chips * per - tiles)], send.at[SPREAD])
            wait_bytes(sorted_pieces.at[pl.ds(0, ngx - 1), pl.ds(0, tiles)], send.at[GATHER])

    kinds_right.wait_send()
    kinds_left.wait_send()
    for step in range(ITERS):
        for face in started[step]:
            face.wait_send()
        for side, there in ((0, gy < ny - 1), (1, gy > 0)):

            @pl.when(there)
            def _():
                wait_bytes(cols_in.at[step, side], send.at[y_sem(step, side)])

        wait_bytes(sums_a.at[step, pl.ds(0, group_a - 1)], send.at[a_sem(step)])
        wait_bytes(sums_b.at[step, pl.ds(0, group_b - 1)], send.at[b_sem(step)])


def tiles_per_chip(chips):
    return -(-220 // chips)


def solution(mesh):
    ngx, ny = mesh.shape["gx"], mesh.shape["gy"]
    nx, nz = (4, 8) if ngx == 64 else (1, ngx // 2)
    chips = ngx // 2
    per = tiles_per_chip(chips)
    big = (per + 1) // 2
    spare = 2 * big - per

    def per_device(populations, mass, cell_type, bubble_id, slab_source, gas_density):
        vmem = pl.BlockSpec(memory_space=pltpu.VMEM)
        smem = pl.BlockSpec(memory_space=pltpu.SMEM)

        def tiles(count, dtype=F32):
            return pltpu.VMEM((count, 8, 128), dtype)

        g, m, v = pl.pallas_call(
            functools.partial(kernel, (nx, nz, ny)),
            out_shape=(
                jax.ShapeDtypeStruct((190, 8, 128), F32),
                jax.ShapeDtypeStruct((10, 8, 128), F32),
                jax.ShapeDtypeStruct((8, 128), F32),
            ),
            in_specs=[vmem] * 4 + [smem] * 2,
            out_specs=(vmem, vmem, vmem),
            scratch_shapes=[
                tiles(chips * per + spare),
                pltpu.VMEM((ngx, big, 8, 128), F32),
                pltpu.VMEM((ngx, big, 8, 128), F32),
                tiles(chips * per),
                pltpu.VMEM((ITERS, 4, 20, 56, 128), F32),
                pltpu.VMEM((4, 56, 128), F32),
                pltpu.VMEM((19, 10, 8, 128), F32),
                pltpu.VMEM((19, 10, 8, 128), F32),
                pltpu.VMEM((3, 10, 8, 128), F32),
                tiles(10, jnp.int32),
                tiles(10, jnp.int32),
                tiles(10),
                tiles(10),
                tiles(10),
                tiles(10),
                tiles(10),
                tiles(10),
                tiles(BUBBLES),
                pltpu.VMEM((ITERS, 2, 40, 128), F32),
                pltpu.VMEM((ITERS, 2, 3, 40, 128), F32),
                pltpu.VMEM((2, 56, 128), F32),
                pltpu.VMEM((ITERS, nz * 2, 8, 128), F32),
                pltpu.VMEM((ITERS, nx * ny, 8, 128), F32),
                pltpu.VMEM((ITERS, 2, 8, 128), F32),
                pltpu.SemaphoreType.DMA((4 + ITERS * 8,)),
                pltpu.SemaphoreType.DMA((4 + ITERS * 8,)),
            ],
            compiler_params=pltpu.CompilerParams(
                collective_id=0, has_side_effects=True, vmem_limit_bytes=40 * 2**20
            ),
        )(
            populations.reshape(190, 8, 128),
            mass.reshape(10, 8, 128),
            cell_type.reshape(10, 8, 128),
            bubble_id.reshape(10, 8, 128),
            slab_source,
            gas_density,
        )
        return g.reshape(populations.shape), m.reshape(mass.shape), v[0, :BUBBLES]

    return jax.shard_map(
        per_device,
        mesh=mesh,
        in_specs=(
            P(None, "gx", None, "gy"),
            P("gx", None, "gy"),
            P("gx", None, "gy"),
            P("gx", None, "gy"),
            P(),
            P(),
        ),
        out_specs=(P(None, "gx", None, "gy"), P("gx", None, "gy"), P()),
        check_vma=False,
    )
```

time: 566 us -> 107 us (0.19); the launches traced: 557 us -> 107 us
  blocking collectives: 242 us -> 0 us
  Pallas kernels: 0 us -> 100 us
  local copies, waits for them, and re-layouts: 97.1 us -> 6.13 us
  waiting for transfers between devices: 84.7 us -> 0 us
  other arithmetic: 72.1 us -> 0 us
  starting transfers between devices: 38.3 us -> 0 us
  matrix products: 19.9 us -> 0 us
    psum x3 -> x0, blocking collectives: 242 us -> none  [volumes(): return lax.psum(part, ('gx', 'gy'))]
    pallas_call x0 -> x1, Pallas kernels: none -> 100 us  [per_device(): pl.pallas_call(functools.partial(kernel, (nx, nz, ny)), out_shape=(jax.Sh...]
    all_to_all x2 -> x0, waiting for transfers between devices: 64.5 us -> none  [the longest x1 39.1 us: per_device(): lax.all_to_all(pieces, 'gx', split_axis=1, concat_axis=2, tiled=True)]
    unnamed x59 -> x0, other arithmetic: 37.3 us -> none
    unnamed x323 -> x14, local copies, waits for them, and re-layouts: 40.4 us -> 5.61 us
    ppermute x16 -> x0, waiting for transfers between devices: 20.3 us -> none  [the longest x8 13.5 us: with_halo(): lax.ppermute(tail, axis, [(i, (i + 1) % count) for i in range(count)])]
    all_to_all x2 -> x0, starting transfers between devices: 20.1 us -> none  [the longest x1 13.6 us: per_device(): lax.all_to_all(payload.reshape(22, width, depth * across), 'gx', split_ax...]
    dot_general x17 -> x0, matrix products: 19.9 us -> none  [the longest x9 8.26 us: moments(): jnp.einsum('q,q...->...', column, dist, precision=lax.Precision.HIGHEST)]
  transfers between devices with their start and end apart: 18 -> 0, of which waited for: 9 -> 0; matrix products, arithmetic and copies ran while one was open for 5% -> 0% of each run, Pallas kernels for 0% -> 0%
where the time goes in v1:
time: 107 us
  Pallas kernels  100 us (93%)
  local copies, waits for them, and re-layouts  6.13 us (6%)
    pallas_call x1, Pallas kernels, per_device(): pl.pallas_call(functools.partial(kernel, (nx, nz, ny)), out_shape=(jax.Sh...  100 us
    unnamed x14, local copies, waits for them, and re-layouts  5.61 us

profile of v1, /device:TPU:1, one launch (start us, length us, event | category | flops | bytes accessed | tf_op | source)
XLA Modules:
  0.0 106.9 jit_solution(16824116430030050130)
XLA Ops:
  0.6 0.0 copy-start.4
  0.6 0.0 copy-start.5
  0.7 0.6 copy-done.4
  1.3 0.0 copy-done.5
  1.3 0.0 copy-start
  1.3 1.1 %copy-done = f32[19,2,40,128]{3,2,1,0:T(8,128)S(1)} copy-done((f32[19,2,40,128]{3,2,1,0:T(8,128)S(1)}, f32[19,2,40,128]{3,2,1,0:T(8,128)}, u32[]{:S(2)}) %copy-start) | copy-done | bytes 778264
  2.4 0.0 copy-start.1
  2.4 0.8 copy-done.1
  3.2 0.0 copy-start.2
  3.2 0.8 copy-done.2
  4.0 0.0 copy-start.3
  4.0 0.8 copy-done.3
  4.8 100.1 %shard_map.85 = (f32[190,8,128]{2,1,0:T(8,128)S(1)}, f32[10,8,128]{2,1,0:T(8,128)S(1)}, f32[8,128]{1,0:T(8,128)S(1)}) custom-call(f32[190,8,128]{2,1,0:T(8,128)S(1)} %bitcast.8, f32[10,8,128]{2,1,0:T(8,128)S(1)} %bitcast.10, s32[10,8,128]{2,1,0:T(8,128)S(1)} %bitcast.11, s32[10,8,128]{2,1,0:T(8,128)S(1)} %bitcast.12, s32[64]{0:T(128)S(1)} %copy-done.4, ...), custom_call_target="tpu_custom_call" | custom-call | tf_op jit(solution)/shard_map/pallas_call | solution.py:639
  104.9 0.5 slice_bitcast_fusion
  105.4 0.9 copy.11
  106.3 0.6 copy.12
Async XLA Ops:
  0.6 0.7 copy-start.4
  0.6 0.7 copy-start.5
  1.3 1.1 %copy-start = (f32[19,2,40,128]{3,2,1,0:T(8,128)S(1)}, f32[19,2,40,128]{3,2,1,0:T(8,128)}, u32[]{:S(2)}) copy-start(f32[19,2,40,128]{3,2,1,0:T(8,128)} %param.6) | copy-start | bytes 2334724
  2.4 0.8 copy-start.1
  3.2 0.8 copy-start.2
  4.0 0.8 copy-start.3

commit v2 on v1

--- a/solution.py
+++ b/solution.py
@@ -48,20 +48,29 @@
     return (ux, uy, uz, ux + uy, ux - uy, ux + uz, ux - uz, uy + uz, uy - uz)
 
 
+def far_first(size):
+    return sorted(range(size), key=lambda d: -min(d, size - d))
+
+
 def kernel(
     shape,
     pop,
     mass,
     cell,
     label,
-    source,
-    gas_density,
+    source_in,
+    density_in,
     out_g,
     out_m,
     out_v,
     stage,
-    got,
-    sorted_pieces,
+    ints,
+    source,
+    gas_density,
+    got_a,
+    got_b,
+    sorted_a,
+    sorted_b,
     home,
     post,
     kinds,
@@ -80,41 +89,41 @@
     cols_out,
     cols_in,
     cols,
-    sums_a,
-    sums_b,
+    mate_sum,
+    sums,
     part,
+    fetch,
     send,
     recv,
+    row_ready,
 ):
     nx, nz, ny = shape
     ngx = nx * nz * 2
     chips = nx * nz
-    per = tiles_per_chip(chips)
-    big = (per + 1) // 2
-    small = per - big
     gx = lax.axis_index("gx")
     gy = lax.axis_index("gy")
     core = gx % 2
     chip = gx // 2
     pos_x = chip // nz
     pos_z = chip % nz
+    mate = gx + 1 - 2 * core
     right = (gx + 1) % ngx
     left = (gx + ngx - 1) % ngx
     lane = lax.broadcasted_iota(jnp.int32, (8, 128), 1)
 
-    SPREAD, GATHER, KINDS = 0, 1, 2
+    SPREAD, GATHER, KINDS = 0, 2, 4
 
     def x_sem(step, side):
-        return 4 + step * 8 + side
+        return 8 + step * 8 + side
 
     def y_sem(step, side):
-        return 4 + step * 8 + 2 + side
-
-    def a_sem(step):
-        return 4 + step * 8 + 4
-
-    def b_sem(step):
-        return 4 + step * 8 + 5
+        return 8 + step * 8 + 2 + side
+
+    def mate_sem(step):
+        return 8 + step * 8 + 4
+
+    def all_sem(step):
+        return 8 + step * 8 + 5
 
     def remote(src, dst, sem, to_x, to_y):
         return pltpu.make_async_remote_copy(
@@ -129,46 +138,44 @@
     def wait_bytes(ref, sem):
         pltpu.make_async_copy(ref, ref, sem).wait()
 
+    at_x = [lax.rem(pos_x + d, nx) * nz for d in range(nx)]
+    at_z = [lax.rem(pos_z + d, nz) for d in range(nz)]
+    at_y = [lax.rem(gy + d, ny) for d in range(ny)]
+    far_chips = [(dz, dx) for dz in far_first(nz) for dx in far_first(nx)]
+    peers = [
+        (at_x[dx] + at_z[dz], other, dx == dz == 0 and other is core)
+        for dz, dx in far_chips
+        for other in (1 - core, core)
+    ]
+
+    fetches = [
+        pltpu.make_async_copy(src, dst, fetch.at[k])
+        for k, (src, dst) in enumerate(
+            (
+                (cell, ints.at[0:10]),
+                (label, ints.at[10:20]),
+                (pop, stage.at[30:220]),
+                (mass, stage.at[20:30]),
+                (source_in, source),
+                (density_in, gas_density),
+            )
+        )
+    ]
+    for one in fetches:
+        one.start()
+
     barrier = pltpu.get_barrier_semaphore()
 
-    def greet_x(k, carry):
+    for to_chip, to_core, near_by in peers:
+        if not near_by:
+            pl.semaphore_signal(
+                barrier, inc=1, device_id=(to_chip * 2 + to_core, gy), device_id_type=MESH
+            )
+    for k in range(1, ny):
         pl.semaphore_signal(
-            barrier, inc=1, device_id=((gx + k) % ngx, gy), device_id_type=MESH
+            barrier, inc=1, device_id=(gx, (gy + k) % ny), device_id_type=MESH
         )
-        return carry
-
-    lax.fori_loop(1, ngx, greet_x, 0)
-    group_a = nz * 2
-    group_b = nx * ny
-    at_a = gx % group_a
-    at_b = pos_x * ny + gy
-
-    def peer_b(k):
-        other = (at_b + k) % group_b
-        return (other // ny) * group_a + at_a, other % ny
-
-    greeted = ngx - 1
-
-    def greet_b(k, carry):
-        to_x, to_y = peer_b(k)
-
-        @pl.when(to_y != gy)
-        def _():
-            pl.semaphore_signal(barrier, inc=1, device_id=(to_x, to_y), device_id_type=MESH)
-
-        return carry
-
-    lax.fori_loop(1, group_b, greet_b, 0)
-    greeted += group_b - nx
-    for to_x in (left, right):
-        for to_y in ((gy + 1) % ny, (gy + ny - 1) % ny):
-            pl.semaphore_signal(barrier, inc=1, device_id=(to_x, to_y), device_id_type=MESH)
-    greeted += 4
-
-    stage[0:190] = pop[...]
-    stage[190:200] = mass[...]
-    stage[200:210] = cell[...].astype(F32)
-    stage[210:220] = label[...].astype(F32)
+
     walls = jnp.full((PAD, 128), -1.0, F32)
     for slot in range(4):
         kinds[slot, 0:PAD] = walls
@@ -176,80 +183,113 @@
     for side in range(2):
         cols[side, 0:PAD] = walls
         cols[side, PAD + 40 : PAD + 48] = walls
-    pl.semaphore_wait(barrier, greeted)
-
-    def peer_chip(k):
-        dz = (3 * (k // nx) + nz // 2) % nz
-        dx = k % nx
-        return ((pos_x + dx) % nx) * nz + (pos_z + dz) % nz
-
-    def spread(k, carry):
-        to = peer_chip(k)
-        for side, tiles in ((0, big), (1, small)):
-            peer = to * 2 + side
-
-            @pl.when(peer != gx)
+    for one in fetches:
+        one.wait()
+    stage[0:20] = ints[...].astype(F32)
+    pl.semaphore_wait(barrier, ngx - 1 + ny - 1)
+    for k in range(1, ny):
+        pl.semaphore_signal(
+            row_ready, inc=1, device_id=(gx, (gy + k) % ny), device_id_type=MESH
+        )
+
+    chunks = []
+    base = 0
+    for per, got, pieces in zip(chunk_tiles(chips), (got_a, got_b), (sorted_a, sorted_b)):
+        big = (per + 1) // 2
+        chunks.append((base, per, big, ((0, big), (1, per - big)), got, pieces))
+        base += per * chips
+
+    def spread(which):
+        base, per, big, sides, got, pieces = chunks[which]
+
+        for own, _ in sides:
+
+            @pl.when(core == own)
             def _():
-                remote(
-                    stage.at[pl.ds(to * per + side * big, tiles)],
-                    got.at[gx, pl.ds(0, tiles)],
-                    SPREAD,
-                    peer,
-                    gy,
-                ).start()
-
-        return carry
-
-    lax.fori_loop(0, chips, spread, 0)
-    mine = chip * per + core * big
-    got[gx] = stage[pl.ds(mine, big)]
-
-    def take(k, carry):
-        sorted_pieces[k] = got[source[k]]
-        return carry
-
-    for side, tiles in ((0, big), (1, small)):
-
-        @pl.when(core == side)
-        def _():
-            wait_bytes(got.at[pl.ds(0, ngx - 1), pl.ds(0, tiles)], recv.at[SPREAD])
-
-    lax.fori_loop(0, ngx, take, 0, unroll=4)
-
-    def gather(k, carry):
-        to = peer_chip(k)
-        for other in range(2):
-            peer = to * 2 + other
-            for side, tiles in ((0, big), (1, small)):
-
-                @pl.when((peer != gx) & (core == side))
-                def _():
-                    remote(
-                        sorted_pieces.at[peer, pl.ds(0, tiles)],
-                        home.at[pl.ds(chip * per + side * big, tiles)],
-                        GATHER,
-                        peer,
-                        gy,
-                    ).start()
-
-        return carry
-
-    lax.fori_loop(0, chips, gather, 0)
-    for side, tiles in ((0, big), (1, small)):
-
-        @pl.when(core == side)
-        def _():
-            home[pl.ds(chip * per + side * big, tiles)] = sorted_pieces[gx, 0:tiles]
-            wait_bytes(home.at[pl.ds(0, chips * per - tiles)], recv.at[GATHER])
-
+                for dz, dx in far_chips:
+                    to = at_x[dx] + at_z[dz]
+                    for side, tiles in sides:
+                        if dx == dz == 0 and side == own:
+                            continue
+                        remote(
+                            stage.at[pl.ds(base + to * per + side * big, tiles)],
+                            got.at[gx, pl.ds(0, tiles)],
+                            SPREAD + which,
+                            to * 2 + side,
+                            gy,
+                        ).start()
+
+        got[gx] = stage[pl.ds(base + chip * per + core * big, big)]
+
+    def pick(which):
+        base, per, big, sides, got, pieces = chunks[which]
+        for side, tiles in sides:
+
+            @pl.when(core == side)
+            def _():
+                wait_bytes(got.at[pl.ds(0, ngx - 1), pl.ds(0, tiles)], recv.at[SPREAD + which])
+
+        def one(k, carry):
+            pieces[k] = got[source[k]]
+            return carry
+
+        lax.fori_loop(0, ngx, one, 0, unroll=8)
+
+    def gather(which):
+        base, per, big, sides, got, pieces = chunks[which]
+        for side, tiles in sides:
+
+            @pl.when(core == side)
+            def _():
+                at = pl.ds(base + chip * per + side * big, tiles)
+
+                for dz, dx in far_chips:
+                    for other in range(2):
+                        if dx == dz == 0 and side == other:
+                            continue
+                        peer = (at_x[dx] + at_z[dz]) * 2 + other
+                        remote(
+                            pieces.at[peer, pl.ds(0, tiles)],
+                            home.at[at],
+                            GATHER + which,
+                            peer,
+                            gy,
+                        ).start()
+                home[at] = pieces[gx, 0:tiles]
+
+    def gathered(which):
+        base, per, big, sides, got, pieces = chunks[which]
+        for side, tiles in sides:
+
+            @pl.when(core == side)
+            def _():
+                wait_bytes(
+                    home.at[pl.ds(base, chips * per - tiles)], recv.at[GATHER + which]
+                )
+
+    spread(0)
+    spread(1)
+    pick(0)
+    gather(0)
+    pick(1)
+    gather(1)
+
+    gathered(0)
     for x in range(2):
         for z in range(5):
-            kinds[x + 1, PAD + z * 8 : PAD + z * 8 + 8] = home[200 + x * 5 + z]
+            kinds[x + 1, PAD + z * 8 : PAD + z * 8 + 8] = home[x * 5 + z]
     rows = pl.ds(PAD, 40)
     kinds_right = remote(kinds.at[2, rows], kinds.at[0, rows], KINDS, right, gy)
     kinds_left = remote(kinds.at[1, rows], kinds.at[3, rows], KINDS + 1, left, gy)
     kinds_right.start()
     kinds_left.start()
+    label_now = home[10:20].astype(jnp.int32)
+    bubble[...] = label_now
+    turned = jnp.zeros_like(label_now)
+    for bit in range(6):
+        turned = turned | (((label_now >> bit) & 1) << (5 - bit))
+    reversed_label[...] = turned
+    fluid_mass[...] = home[20:30]
 
     def collide(step, i, g):
         x, z = i // 5, i % 5
@@ -304,7 +344,9 @@
         )
         plus.start()
         minus.start()
-
+        return plus, minus
+
+    def send_columns(step):
         def pack(z, carry):
             at = pl.ds(pl.multiple_of(PAD + z * 8, 8), 8)
             up = jnp.zeros((8, 128), F32)
@@ -324,7 +366,7 @@
             cols_out[step, 1, to] = down
             return carry
 
-        lax.fori_loop(0, 5, pack, 0)
+        lax.fori_loop(0, 5, pack, 0, unroll=5)
         for side, there, to_y in ((0, gy < ny - 1, gy + 1), (1, gy > 0, gy - 1)):
 
             @pl.when(there)
@@ -338,8 +380,6 @@
                         to_y,
                     ).start()
 
-        return plus, minus
-
     def wait_columns(step):
         for side, there in ((0, gy > 0), (1, gy < ny - 1)):
 
@@ -358,7 +398,7 @@
                 )
                 return carry
 
-            lax.fori_loop(0, 5, merge, 0)
+            lax.fori_loop(0, 5, merge, 0, unroll=5)
 
     def shifted(value, step_y, j, slot, at, outside):
         if step_y == 0:
@@ -463,52 +503,44 @@
         now = now[0]
         return now + pltpu.roll(now, 64, 1)
 
-    def send_sums(dst, own, sem, step, stage_no, count, peer_of):
-        def one(k, carry):
-            to_x, to_y = peer_of(k)
-            remote(part.at[step, stage_no], dst.at[step, own], sem, to_x, to_y).start()
-            return carry
-
-        lax.fori_loop(1, count, one, 0)
-
-    def peer_a(k):
-        return gx - at_a + (at_a + k) % group_a, gy
-
     def begin_sum(step, value):
-        part[step, 0] = value
-        sums_a[step, at_a] = value
-        send_sums(sums_a, at_a, a_sem(step), step, 0, group_a, peer_a)
+        part[step, 0] = jnp.sum(value, axis=0, keepdims=True)
+        remote(part.at[step, 0], mate_sum.at[step], mate_sem(step), mate, gy).start()
 
     def middle_sum(step):
-        wait_bytes(sums_a.at[step, pl.ds(0, group_a - 1)], recv.at[a_sem(step)])
-        value = jnp.sum(sums_a[step], axis=0)
+        wait_bytes(mate_sum.at[step], recv.at[mate_sem(step)])
+        value = part[step, 0] + mate_sum[step]
         part[step, 1] = value
-        sums_b[step, at_b] = value
-        send_sums(sums_b, at_b, b_sem(step), step, 1, group_b, peer_b)
+        mine = chip * ny + gy
+        sums[step, mine] = value
+
+        for dz, dx in far_chips:
+            to_x = (at_x[dx] + at_z[dz]) * 2 + core
+            for dy in far_first(ny):
+                if dx == dy == dz == 0:
+                    continue
+                remote(
+                    part.at[step, 1], sums.at[step, mine], all_sem(step), to_x, at_y[dy]
+                ).start()
 
     def end_sum(step):
-        wait_bytes(sums_b.at[step, pl.ds(0, group_b - 1)], recv.at[b_sem(step)])
-        value = jnp.sum(jnp.sum(sums_b[step], axis=0), axis=0, keepdims=True)
-        return jnp.broadcast_to(value, (8, 128))
+        wait_bytes(sums.at[step, pl.ds(0, chips * ny - 1)], recv.at[all_sem(step)])
+        return jnp.broadcast_to(jnp.sum(sums[step], axis=0), (8, 128))
 
     def first(i, carry):
-        rho = collide(0, i, [home[q * 10 + i] for q in range(19)])
-        kind = home[200 + i]
-        phi, part_gas = level(kind, home[190 + i], rho)
+        rho = collide(0, i, [home[30 + q * 10 + i] for q in range(19)])
+        kind = home[i]
+        phi, part_gas = level(kind, fluid_mass[i], rho)
         put_half(0, i, phi)
         share[i] = part_gas
-        fluid_mass[i] = home[190 + i]
         return carry
 
+    gathered(1)
     lax.fori_loop(0, 10, first, 0)
+    pl.semaphore_wait(row_ready, ny - 1)
     faces = send_faces(0)
+    send_columns(0)
     started = [faces]
-    label_now = home[210:220].astype(jnp.int32)
-    bubble[...] = label_now
-    turned = jnp.zeros_like(label_now)
-    for bit in range(6):
-        turned = turned | (((label_now >> bit) & 1) << (5 - bit))
-    reversed_label[...] = turned
     volume_start = member_sums()
     bubble_lane = lane & (BUBBLES - 1)
     table = jnp.zeros((8, 128), F32)
@@ -536,7 +568,7 @@
     for step in range(ITERS):
 
         def settle(i, carry):
-            kind = home[200 + i]
+            kind = home[i]
             rho = base_rho[i] + gas_here[i] * gas_rho[i]
             liquid_mass = jnp.where(
                 kind == 1.0, fluid_mass[i] + gain[i], jnp.where(kind == 2.0, rho, 0.0)
@@ -564,6 +596,7 @@
             faces = send_faces(step + 1)
             started.append(faces)
             middle_sum(step)
+            send_columns(step + 1)
             wait_columns(step + 1)
             for face in faces:
                 face.wait_recv()
@@ -585,7 +618,7 @@
         lookup(density_start * start_total / total)
 
     def finish(i, carry):
-        gas = home[200 + i] == 0.0
+        gas = home[i] == 0.0
         density = gas_here[i]
         for q in range(19):
             out_g[q * 10 + i] = jnp.where(gas, density, out_g[q * 10 + i])
@@ -595,12 +628,16 @@
     out_m[...] = fluid_mass[...]
     out_v[...] = total * (BUBBLES / (ngx * ny * 2 * 40 * 128))
 
-    for side, tiles in ((0, big), (1, small)):
-
-        @pl.when(core == side)
-        def _():
-            wait_bytes(stage.at[pl.ds(0, chips * per - tiles)], send.at[SPREAD])
-            wait_bytes(sorted_pieces.at[pl.ds(0, ngx - 1), pl.ds(0, tiles)], send.at[GATHER])
+    for which in range(2):
+        base, per, big, sides, got, pieces = chunks[which]
+        for side, tiles in sides:
+
+            @pl.when(core == side)
+            def _():
+                wait_bytes(stage.at[pl.ds(0, chips * per - tiles)], send.at[SPREAD + which])
+                wait_bytes(
+                    pieces.at[pl.ds(0, ngx - 1), pl.ds(0, tiles)], send.at[GATHER + which]
+                )
 
     kinds_right.wait_send()
     kinds_left.wait_send()
@@ -613,25 +650,25 @@
             def _():
                 wait_bytes(cols_in.at[step, side], send.at[y_sem(step, side)])
 
-        wait_bytes(sums_a.at[step, pl.ds(0, group_a - 1)], send.at[a_sem(step)])
-        wait_bytes(sums_b.at[step, pl.ds(0, group_b - 1)], send.at[b_sem(step)])
-
-
-def tiles_per_chip(chips):
-    return -(-220 // chips)
+        wait_bytes(mate_sum.at[step], send.at[mate_sem(step)])
+        wait_bytes(sums.at[step, pl.ds(0, chips * ny - 1)], send.at[all_sem(step)])
+
+
+def chunk_tiles(chips):
+    per = -(-220 // chips)
+    return (per * 4 + 6) // 7, per - (per * 4 + 6) // 7
 
 
 def solution(mesh):
     ngx, ny = mesh.shape["gx"], mesh.shape["gy"]
     nx, nz = (4, 8) if ngx == 64 else (1, ngx // 2)
     chips = ngx // 2
-    per = tiles_per_chip(chips)
-    big = (per + 1) // 2
-    spare = 2 * big - per
+    per_a, per_b = chunk_tiles(chips)
+    big_a, big_b = (per_a + 1) // 2, (per_b + 1) // 2
 
     def per_device(populations, mass, cell_type, bubble_id, slab_source, gas_density):
         vmem = pl.BlockSpec(memory_space=pltpu.VMEM)
-        smem = pl.BlockSpec(memory_space=pltpu.SMEM)
+        hbm = pl.BlockSpec(memory_space=pltpu.HBM)
 
         def tiles(count, dtype=F32):
             return pltpu.VMEM((count, 8, 128), dtype)
@@ -643,13 +680,18 @@
                 jax.ShapeDtypeStruct((10, 8, 128), F32),
                 jax.ShapeDtypeStruct((8, 128), F32),
             ),
-            in_specs=[vmem] * 4 + [smem] * 2,
+            in_specs=[hbm] * 6,
             out_specs=(vmem, vmem, vmem),
             scratch_shapes=[
-                tiles(chips * per + spare),
-                pltpu.VMEM((ngx, big, 8, 128), F32),
-                pltpu.VMEM((ngx, big, 8, 128), F32),
-                tiles(chips * per),
+                tiles(chips * (per_a + per_b) + 1),
+                tiles(20, jnp.int32),
+                pltpu.SMEM((ngx,), jnp.int32),
+                pltpu.SMEM((BUBBLES,), F32),
+                pltpu.VMEM((ngx, big_a, 8, 128), F32),
+                pltpu.VMEM((ngx, big_b, 8, 128), F32),
+                pltpu.VMEM((ngx, big_a, 8, 128), F32),
+                pltpu.VMEM((ngx, big_b, 8, 128), F32),
+                tiles(chips * (per_a + per_b)),
                 pltpu.VMEM((ITERS, 4, 20, 56, 128), F32),
                 pltpu.VMEM((4, 56, 128), F32),
                 pltpu.VMEM((19, 10, 8, 128), F32),
@@ -667,11 +709,13 @@
                 pltpu.VMEM((ITERS, 2, 40, 128), F32),
                 pltpu.VMEM((ITERS, 2, 3, 40, 128), F32),
                 pltpu.VMEM((2, 56, 128), F32),
-                pltpu.VMEM((ITERS, nz * 2, 8, 128), F32),
-                pltpu.VMEM((ITERS, nx * ny, 8, 128), F32),
-                pltpu.VMEM((ITERS, 2, 8, 128), F32),
-                pltpu.SemaphoreType.DMA((4 + ITERS * 8,)),
-                pltpu.SemaphoreType.DMA((4 + ITERS * 8,)),
+                pltpu.VMEM((ITERS, 1, 128), F32),
+                pltpu.VMEM((ITERS, chips * ny, 1, 128), F32),
+                pltpu.VMEM((ITERS, 2, 1, 128), F32),
+                pltpu.SemaphoreType.DMA((6,)),
+                pltpu.SemaphoreType.DMA((8 + ITERS * 8,)),
+                pltpu.SemaphoreType.DMA((8 + ITERS * 8,)),
+                pltpu.SemaphoreType.REGULAR,
             ],
             compiler_params=pltpu.CompilerParams(
                 collective_id=0, has_side_effects=True, vmem_limit_bytes=40 * 2**20

time: 107 us -> 99.6 us (0.931)
  Pallas kernels: 100 us -> 92.5 us
    pallas_call x1, Pallas kernels: 100 us -> 92.5 us  [per_device(): pl.pallas_call(functools.partial(kernel, (nx, nz, ny)), out_shape=(jax.Sh...]
where the time goes in v2:
time: 99.6 us; the launch traced here: 99.3 us
  Pallas kernels  92.5 us (93%)
  local copies, waits for them, and re-layouts  6.13 us (6%)
    pallas_call x1, Pallas kernels, per_device(): pl.pallas_call(functools.partial(kernel, (nx, nz, ny)), out_shape=(jax.Sh...  92.5 us
    unnamed x14, local copies, waits for them, and re-layouts  5.61 us

profile of v2, /device:TPU:1, one launch (start us, length us, event | category | flops | bytes accessed | tf_op | source)
XLA Modules:
  0.0 99.3 jit_solution(18246003139774777824)
XLA Ops:
  0.6 0.0 copy-start.4
  0.6 0.0 copy-start.5
  0.7 0.6 copy-done.4
  1.3 0.0 copy-done.5
  1.3 0.0 copy-start
  1.3 1.1 %copy-done = f32[19,2,40,128]{3,2,1,0:T(8,128)S(1)} copy-done((f32[19,2,40,128]{3,2,1,0:T(8,128)S(1)}, f32[19,2,40,128]{3,2,1,0:T(8,128)}, u32[]{:S(2)}) %copy-start) | copy-done | bytes 778264
  2.4 0.0 copy-start.1
  2.4 0.8 copy-done.1
  3.2 0.0 copy-start.2
  3.2 0.8 copy-done.2
  4.0 0.0 copy-start.3
  4.0 0.8 copy-done.3
  4.8 92.5 %shard_map.85 = (f32[190,8,128]{2,1,0:T(8,128)S(1)}, f32[10,8,128]{2,1,0:T(8,128)S(1)}, f32[8,128]{1,0:T(8,128)S(1)}) custom-call(f32[190,8,128]{2,1,0:T(8,128)S(1)} %bitcast.8, f32[10,8,128]{2,1,0:T(8,128)S(1)} %bitcast.10, s32[10,8,128]{2,1,0:T(8,128)S(1)} %bitcast.11, s32[10,8,128]{2,1,0:T(8,128)S(1)} %bitcast.12, s32[64]{0:T(128)S(1)} %copy-done.4, ...), custom_call_target="tpu_custom_call" | custom-call | tf_op jit(solution)/shard_map/pallas_call | solution.py:676
  97.3 0.5 slice_bitcast_fusion
  97.8 0.9 copy.11
  98.7 0.6 copy.12
Async XLA Ops:
  0.6 0.7 copy-start.4
  0.6 0.7 copy-start.5
  1.3 1.1 %copy-start = (f32[19,2,40,128]{3,2,1,0:T(8,128)S(1)}, f32[19,2,40,128]{3,2,1,0:T(8,128)}, u32[]{:S(2)}) copy-start(f32[19,2,40,128]{3,2,1,0:T(8,128)} %param.6) | copy-start | bytes 2334724
  2.4 0.8 copy-start.1
  3.2 0.8 copy-start.2
  4.0 0.8 copy-start.3

commit v3 on v2

--- a/solution.py
+++ b/solution.py
@@ -10,6 +10,7 @@
 BUBBLES = 64
 ITERS = 3
 OMEGA = 1.6
+VMEM_LIMIT = 56 * 2**20
 MESH = pl.DeviceIdType.MESH
 F32 = jnp.float32
 
@@ -37,9 +38,8 @@
 HALF = 19
 ORDER = (1, 7, 9, 11, 13, HALF, 2, 8, 10, 12, 14, 0, 3, 4, 5, 6, 15, 16, 17, 18)
 AT = {field: pos for pos, field in enumerate(ORDER)}
-KIND = 20
-COLS_UP = (3, 7, 10, 15, 17, HALF, KIND)
-COLS_DOWN = (4, 8, 9, 16, 18, HALF, KIND)
+COLS_UP = (3, 7, 10, 15, 17, HALF)
+COLS_DOWN = (4, 8, 9, 16, 18, HALF)
 PAIRS = ((1, 2), (3, 4), (5, 6), (7, 8), (9, 10), (11, 12), (13, 14), (15, 16), (17, 18))
 PAD = 8
 
@@ -89,6 +89,9 @@
     cols_out,
     cols_in,
     cols,
+    kind_cols_out,
+    kind_cols_in,
+    kind_cols,
     mate_sum,
     sums,
     part,
@@ -148,6 +151,59 @@
         for other in (1 - core, core)
     ]
 
+    def send_columns(out, into, sem, up_fields, down_fields):
+        for z in range(5):
+            up = jnp.zeros((8, 128), F32)
+            down = jnp.zeros((8, 128), F32)
+            for j, (high, low) in enumerate(zip(up_fields, down_fields)):
+                for x in range(2):
+                    spot = j * 4 + x + 1
+                    at = pl.ds(PAD + z * 8, 8)
+                    up = jnp.where(lane == spot, pltpu.roll(high(x + 1, at), spot + 1, 1), up)
+                    down = jnp.where(lane == spot, pltpu.roll(low(x + 1, at), spot, 1), down)
+            out[0, z * 8 : z * 8 + 8] = up
+            out[1, z * 8 : z * 8 + 8] = down
+        for side, there, to_y in ((0, gy < ny - 1, gy + 1), (1, gy > 0, gy - 1)):
+
+            @pl.when(there)
+            def _():
+                for shift, to_x in ((-1, left), (0, gx), (1, right)):
+                    remote(out.at[side], into.at[side, 1 - shift], sem + side, to_x, to_y).start()
+
+    def wait_columns(into, whole, sem):
+        for side, there in ((0, gy > 0), (1, gy < ny - 1)):
+
+            @pl.when(there)
+            def _():
+                wait_bytes(into.at[side], recv.at[sem + side])
+
+        slot = lane % 4
+        for side in range(2):
+            for z in range(5):
+                of = pl.ds(z * 8, 8)
+                before = pltpu.roll(into[side, 0, of], 126, 1)
+                after = pltpu.roll(into[side, 2, of], 2, 1)
+                whole[side, PAD + z * 8 : PAD + z * 8 + 8] = jnp.where(
+                    slot == 0, before, jnp.where(slot == 3, after, into[side, 1, of])
+                )
+
+    def columns_sent(into, sem):
+        for side, there in ((0, gy < ny - 1), (1, gy > 0)):
+
+            @pl.when(there)
+            def _():
+                wait_bytes(into.at[side], send.at[sem + side])
+
+    def post_columns(step):
+        def fields(order):
+            return [
+                lambda slot, at, f=f: post[step, slot, AT[f], at] for f in order
+            ]
+
+        send_columns(
+            cols_out.at[step], cols_in.at[step], y_sem(step, 0), fields(COLS_UP), fields(COLS_DOWN)
+        )
+
     fetches = [
         pltpu.make_async_copy(src, dst, fetch.at[k])
         for k, (src, dst) in enumerate(
@@ -181,8 +237,9 @@
         kinds[slot, 0:PAD] = walls
         kinds[slot, PAD + 40 : PAD + 48] = walls
     for side in range(2):
-        cols[side, 0:PAD] = walls
-        cols[side, PAD + 40 : PAD + 48] = walls
+        for edge in (cols, kind_cols):
+            edge[side, 0:PAD] = walls
+            edge[side, PAD + 40 : PAD + 48] = walls
     for one in fetches:
         one.wait()
     stage[0:20] = ints[...].astype(F32)
@@ -283,6 +340,9 @@
     kinds_left = remote(kinds.at[1, rows], kinds.at[3, rows], KINDS + 1, left, gy)
     kinds_right.start()
     kinds_left.start()
+    pl.semaphore_wait(row_ready, ny - 1)
+    kind_fields = [lambda slot, at: kinds[slot, at]]
+    send_columns(kind_cols_out, kind_cols_in, KINDS + 2, kind_fields, kind_fields)
     label_now = home[10:20].astype(jnp.int32)
     bubble[...] = label_now
     turned = jnp.zeros_like(label_now)
@@ -346,61 +406,7 @@
         minus.start()
         return plus, minus
 
-    def send_columns(step):
-        def pack(z, carry):
-            at = pl.ds(pl.multiple_of(PAD + z * 8, 8), 8)
-            up = jnp.zeros((8, 128), F32)
-            down = jnp.zeros((8, 128), F32)
-            for j in range(7 if step == 0 else 6):
-                for x in range(2):
-                    spot = j * 4 + x + 1
-                    if COLS_UP[j] == KIND:
-                        high = low = kinds[x + 1, at]
-                    else:
-                        high = post[step, x + 1, AT[COLS_UP[j]], at]
-                        low = post[step, x + 1, AT[COLS_DOWN[j]], at]
-                    up = jnp.where(lane == spot, pltpu.roll(high, spot + 1, 1), up)
-                    down = jnp.where(lane == spot, pltpu.roll(low, spot, 1), down)
-            to = pl.ds(pl.multiple_of(z * 8, 8), 8)
-            cols_out[step, 0, to] = up
-            cols_out[step, 1, to] = down
-            return carry
-
-        lax.fori_loop(0, 5, pack, 0, unroll=5)
-        for side, there, to_y in ((0, gy < ny - 1, gy + 1), (1, gy > 0, gy - 1)):
-
-            @pl.when(there)
-            def _():
-                for shift, to_x in ((-1, left), (0, gx), (1, right)):
-                    remote(
-                        cols_out.at[step, side],
-                        cols_in.at[step, side, 1 - shift],
-                        y_sem(step, side),
-                        to_x,
-                        to_y,
-                    ).start()
-
-    def wait_columns(step):
-        for side, there in ((0, gy > 0), (1, gy < ny - 1)):
-
-            @pl.when(there)
-            def _():
-                wait_bytes(cols_in.at[step, side], recv.at[y_sem(step, side)])
-
-            def merge(z, carry):
-                of = pl.ds(pl.multiple_of(z * 8, 8), 8)
-                before = pltpu.roll(cols_in[step, side, 0, of], 126, 1)
-                after = pltpu.roll(cols_in[step, side, 2, of], 2, 1)
-                slot = lane % 4
-                here = cols_in[step, side, 1, of]
-                cols[side, pl.ds(pl.multiple_of(PAD + z * 8, 8), 8)] = jnp.where(
-                    slot == 0, before, jnp.where(slot == 3, after, here)
-                )
-                return carry
-
-            lax.fori_loop(0, 5, merge, 0, unroll=5)
-
-    def shifted(value, step_y, j, slot, at, outside):
+    def shifted(value, cols, step_y, j, slot, at, outside):
         if step_y == 0:
             return value
         if step_y == 1:
@@ -420,7 +426,9 @@
             step_x, step_y, step_z = LATTICE[d]
             slot = x + 1 - step_x
             at = pl.ds(row - step_z, 8)
-            near[d, i] = shifted(kinds[slot, at], step_y, 6, slot, at, (gy == 0, gy == ny - 1))
+            near[d, i] = shifted(
+                kinds[slot, at], kind_cols, step_y, 0, slot, at, (gy == 0, gy == ny - 1)
+            )
         return carry
 
     def twice_even(i):
@@ -447,8 +455,8 @@
                 slot = x + 1 - step_x
                 at = pl.ds(row - step_z, 8)
                 j = 0 if step_y == 0 else (COLS_UP if step_y == 1 else COLS_DOWN).index(d)
-                came = shifted(post[step, slot, AT[d], at], step_y, j, slot, at, None)
-                near_half = shifted(post[step, slot, AT[HALF], at], step_y, 5, slot, at, None)
+                came = shifted(post[step, slot, AT[d], at], cols, step_y, j, slot, at, None)
+                near_half = shifted(post[step, slot, AT[HALF], at], cols, step_y, 5, slot, at, None)
                 kind = near[d, i]
                 bounced = here[back]
                 value = jnp.where(kind >= 1.0, came, bounced)
@@ -487,8 +495,14 @@
         lax.fori_loop(0, 10, one, 0, unroll=5)
 
     def member_sums():
+        labels = [reversed_label[i] for i in range(10)]
+        shares = [share[i] for i in range(10)]
+
         def one(b, carry):
-            members[b] = jnp.sum(jnp.where(reversed_label[...] == b, share[...], 0.0), axis=0)
+            parts = [jnp.where(which == b, part_of, 0.0) for which, part_of in zip(labels, shares)]
+            while len(parts) > 1:
+                parts = [sum(parts[k : k + 2]) for k in range(0, len(parts), 2)]
+            members[b] = parts[0]
             return carry
 
         lax.fori_loop(0, BUBBLES, one, 0, unroll=8)
@@ -535,13 +549,6 @@
         share[i] = part_gas
         return carry
 
-    gathered(1)
-    lax.fori_loop(0, 10, first, 0)
-    pl.semaphore_wait(row_ready, ny - 1)
-    faces = send_faces(0)
-    send_columns(0)
-    started = [faces]
-    volume_start = member_sums()
     bubble_lane = lane & (BUBBLES - 1)
     table = jnp.zeros((8, 128), F32)
     for b in range(BUBBLES):
@@ -549,10 +556,17 @@
     density_start = table
     lookup(table)
 
+    gathered(1)
+    lax.fori_loop(0, 10, first, 0)
+    faces = send_faces(0)
+    post_columns(0)
+    started = [faces]
     kinds_right.wait_recv()
     kinds_left.wait_recv()
-    wait_columns(0)
+    wait_columns(kind_cols_in, kind_cols, KINDS + 2)
     lax.fori_loop(0, 10, find_near, 0)
+    volume_start = member_sums()
+    wait_columns(cols_in.at[0], cols, y_sem(0, 0))
     for face in faces:
         face.wait_recv()
 
@@ -596,8 +610,8 @@
             faces = send_faces(step + 1)
             started.append(faces)
             middle_sum(step)
-            send_columns(step + 1)
-            wait_columns(step + 1)
+            post_columns(step + 1)
+            wait_columns(cols_in.at[step + 1], cols, y_sem(step + 1, 0))
             for face in faces:
                 face.wait_recv()
             stream_all(step + 1)
@@ -626,7 +640,7 @@
 
     lax.fori_loop(0, 10, finish, 0)
     out_m[...] = fluid_mass[...]
-    out_v[...] = total * (BUBBLES / (ngx * ny * 2 * 40 * 128))
+    out_v[...] = total[0:1, :BUBBLES] * (BUBBLES / (ngx * ny * 2 * 40 * 128))
 
     for which in range(2):
         base, per, big, sides, got, pieces = chunks[which]
@@ -641,17 +655,31 @@
 
     kinds_right.wait_send()
     kinds_left.wait_send()
+    columns_sent(kind_cols_in, KINDS + 2)
     for step in range(ITERS):
         for face in started[step]:
             face.wait_send()
-        for side, there in ((0, gy < ny - 1), (1, gy > 0)):
-
-            @pl.when(there)
-            def _():
-                wait_bytes(cols_in.at[step, side], send.at[y_sem(step, side)])
-
+        columns_sent(cols_in.at[step], y_sem(step, 0))
         wait_bytes(mate_sum.at[step], send.at[mate_sem(step)])
         wait_bytes(sums.at[step, pl.ds(0, chips * ny - 1)], send.at[all_sem(step)])
+
+
+def hand_over(g, m, v, out_g, out_m, out_v, held_g, held_m, held_v, sem):
+    parts = [
+        (g.at[pl.ds(k * 38, 38)], held_g.at[pl.ds(k * 38, 38)], out_g.at[pl.ds(k * 38, 38)])
+        for k in range(5)
+    ]
+    parts.append((m, held_m, out_m))
+    parts.append((v, held_v, out_v))
+    inward = [pltpu.make_async_copy(p[0], p[1], sem.at[0, k]) for k, p in enumerate(parts)]
+    outward = [pltpu.make_async_copy(p[1], p[2], sem.at[1, k]) for k, p in enumerate(parts)]
+    for one in inward:
+        one.start()
+    for one, other in zip(inward, outward):
+        one.wait()
+        other.start()
+    for one in outward:
+        one.wait()
 
 
 def chunk_tiles(chips):
@@ -678,7 +706,7 @@
             out_shape=(
                 jax.ShapeDtypeStruct((190, 8, 128), F32),
                 jax.ShapeDtypeStruct((10, 8, 128), F32),
-                jax.ShapeDtypeStruct((8, 128), F32),
+                jax.ShapeDtypeStruct((1, BUBBLES), F32),
             ),
             in_specs=[hbm] * 6,
             out_specs=(vmem, vmem, vmem),
@@ -709,6 +737,9 @@
                 pltpu.VMEM((ITERS, 2, 40, 128), F32),
                 pltpu.VMEM((ITERS, 2, 3, 40, 128), F32),
                 pltpu.VMEM((2, 56, 128), F32),
+                pltpu.VMEM((2, 40, 128), F32),
+                pltpu.VMEM((2, 3, 40, 128), F32),
+                pltpu.VMEM((2, 56, 128), F32),
                 pltpu.VMEM((ITERS, 1, 128), F32),
                 pltpu.VMEM((ITERS, chips * ny, 1, 128), F32),
                 pltpu.VMEM((ITERS, 2, 1, 128), F32),
@@ -718,7 +749,7 @@
                 pltpu.SemaphoreType.REGULAR,
             ],
             compiler_params=pltpu.CompilerParams(
-                collective_id=0, has_side_effects=True, vmem_limit_bytes=40 * 2**20
+                collective_id=0, has_side_effects=True, vmem_limit_bytes=VMEM_LIMIT
             ),
         )(
             populations.reshape(190, 8, 128),
@@ -728,7 +759,25 @@
             slab_source,
             gas_density,
         )
-        return g.reshape(populations.shape), m.reshape(mass.shape), v[0, :BUBBLES]
+        anywhere = pl.BlockSpec(memory_space=pl.ANY)
+        g, m, v = pl.pallas_call(
+            hand_over,
+            out_shape=(
+                jax.ShapeDtypeStruct((190, 8, 128), F32),
+                jax.ShapeDtypeStruct((10, 8, 128), F32),
+                jax.ShapeDtypeStruct((1, BUBBLES), F32),
+            ),
+            in_specs=[anywhere] * 3,
+            out_specs=(hbm, hbm, hbm),
+            scratch_shapes=[
+                tiles(190),
+                tiles(10),
+                pltpu.VMEM((1, BUBBLES), F32),
+                pltpu.SemaphoreType.DMA((2, 7)),
+            ],
+            compiler_params=pltpu.CompilerParams(vmem_limit_bytes=VMEM_LIMIT),
+        )(g, m, v)
+        return g.reshape(populations.shape), m.reshape(mass.shape), v.reshape(BUBBLES)
 
     return jax.shard_map(
         per_device,

time: 99.6 us -> 94.9 us (0.953)
  local copies, waits for them, and re-layouts: 6.13 us -> 0 us
  Pallas kernels: 92.5 us -> 94.2 us
    unnamed x14 -> x0, local copies, waits for them, and re-layouts: 5.61 us -> none
    pallas_call x0 -> x1, Pallas kernels: none -> 2.01 us  [per_device(): pl.pallas_call(hand_over, out_shape=(jax.ShapeDtypeStruct((190, 8, 128),...]
where the time goes in v3:
time: 94.9 us; the launch traced here: 94.8 us
  Pallas kernels  94.2 us (99%)
    pallas_call x1, Pallas kernels, per_device(): pl.pallas_call(functools.partial(kernel, (nx, nz, ny)), out_shape=(jax.Sh...  92.1 us
    pallas_call x1, Pallas kernels, per_device(): pl.pallas_call(hand_over, out_shape=(jax.ShapeDtypeStruct((190, 8, 128),...  2.01 us

profile of v3, /device:TPU:1, one launch (start us, length us, event | category | flops | bytes accessed | tf_op | source)
XLA Modules:
  0.0 94.8 jit_solution(13565176247472595942)
XLA Ops:
  0.6 92.1 %shard_map.85 = (f32[190,8,128]{2,1,0:T(8,128)}, f32[10,8,128]{2,1,0:T(8,128)}, f32[1,64]{1,0:T(1,128)}) custom-call(f32[190,8,128]{2,1,0:T(8,128)} %bitcast.7, f32[10,8,128]{2,1,0:T(8,128)} %bitcast.8, s32[10,8,128]{2,1,0:T(8,128)} %bitcast.9, s32[10,8,128]{2,1,0:T(8,128)} %bitcast.10, s32[64]{0:T(128)} %source_in.1, f32[64]{0:T(128)} %density_in.1), custom_call_target="tpu_custom_call" | custom-call | tf_op jit(solution)/shard_map/pallas_call | solution.py:704
  92.8 2.0 %shard_map.86 = (f32[190,8,128]{2,1,0:T(8,128)}, f32[10,8,128]{2,1,0:T(8,128)}, f32[1,64]{1,0:T(1,128)}) custom-call(f32[190,8,128]{2,1,0:T(8,128)} %get-tuple-element.9.g, f32[10,8,128]{2,1,0:T(8,128)} %get-tuple-element.10.m, f32[1,64]{1,0:T(1,128)} %get-tuple-element.11.v), custom_call_target="tpu_custom_call" | custom-call | tf_op jit(solution)/shard_map/pallas_call | solution.py:763

commit v4 on v3

--- a/solution.py
+++ b/solution.py
@@ -78,14 +78,12 @@
     waiting,
     speed,
     bubble,
-    reversed_label,
     fluid_mass,
     share,
     base_rho,
     gas_rho,
     gain,
     gas_here,
-    members,
     cols_out,
     cols_in,
     cols,
@@ -343,12 +341,7 @@
     pl.semaphore_wait(row_ready, ny - 1)
     kind_fields = [lambda slot, at: kinds[slot, at]]
     send_columns(kind_cols_out, kind_cols_in, KINDS + 2, kind_fields, kind_fields)
-    label_now = home[10:20].astype(jnp.int32)
-    bubble[...] = label_now
-    turned = jnp.zeros_like(label_now)
-    for bit in range(6):
-        turned = turned | (((label_now >> bit) & 1) << (5 - bit))
-    reversed_label[...] = turned
+    bubble[...] = home[10:20].astype(jnp.int32)
     fluid_mass[...] = home[20:30]
 
     def collide(step, i, g):
@@ -495,26 +488,26 @@
         lax.fori_loop(0, 10, one, 0, unroll=5)
 
     def member_sums():
-        labels = [reversed_label[i] for i in range(10)]
+        labels = [bubble[i] for i in range(10)]
         shares = [share[i] for i in range(10)]
 
-        def one(b, carry):
+        def one(b):
             parts = [jnp.where(which == b, part_of, 0.0) for which, part_of in zip(labels, shares)]
             while len(parts) > 1:
                 parts = [sum(parts[k : k + 2]) for k in range(0, len(parts), 2)]
-            members[b] = parts[0]
-            return carry
-
-        lax.fori_loop(0, BUBBLES, one, 0, unroll=8)
-        now = members[...]
-        for bit in range(6):
-            half = now.shape[0] // 2
-            first, second = now[:half], now[half:]
-            odd = ((lax.broadcasted_iota(jnp.int32, first.shape, 2) >> bit) & 1) == 1
+            return parts[0]
+
+        def merged(bits, b):
+            if bits == 0:
+                return one(b)
+            bit = bits - 1
+            first, second = merged(bit, b), merged(bit, b + (1 << bit))
+            odd = (lane >> bit) & 1 == 1
             keep = jnp.where(odd, second, first)
             move = jnp.where(odd, first, second)
-            now = keep + pltpu.roll(move, 128 - (1 << bit), 2)
-        now = now[0]
+            return keep + pltpu.roll(move, 128 - (1 << bit), 1)
+
+        now = merged(6, 0)
         return now + pltpu.roll(now, 64, 1)
 
     def begin_sum(step, value):
@@ -575,7 +568,7 @@
             stream(step, i)
             return carry
 
-        lax.fori_loop(0, 10, one, 0)
+        lax.fori_loop(0, 10, one, 0, unroll=5)
 
     stream_all(0)
     start_total = None
@@ -619,11 +612,13 @@
 
             def last(i, carry):
                 for q, value in enumerate(arrived(i)):
-                    out_g[q * 10 + i] = value
+                    waiting[q, i] = value
                 return carry
 
             lax.fori_loop(0, 10, last, 0)
             middle_sum(step)
+            store_g = pltpu.make_async_copy(waiting, out_g, fetch.at[0])
+            store_g.start()
         total = end_sum(step)
         if step == 0:
             other = pltpu.roll(total, 64, 1)
@@ -631,17 +626,12 @@
             total = jnp.where(lane < BUBBLES, total, other)
         lookup(density_start * start_total / total)
 
-    def finish(i, carry):
-        gas = home[i] == 0.0
-        density = gas_here[i]
-        for q in range(19):
-            out_g[q * 10 + i] = jnp.where(gas, density, out_g[q * 10 + i])
-        return carry
-
-    lax.fori_loop(0, 10, finish, 0)
-    out_m[...] = fluid_mass[...]
+    out_m[0:10] = fluid_mass[...]
+    out_m[10:20] = home[0:10]
+    out_m[20:30] = gas_here[...]
     out_v[...] = total[0:1, :BUBBLES] * (BUBBLES / (ngx * ny * 2 * 40 * 128))
 
+    store_g.wait()
     for which in range(2):
         base, per, big, sides, got, pieces = chunks[which]
         for side, tiles in sides:
@@ -665,19 +655,32 @@
 
 
 def hand_over(g, m, v, out_g, out_m, out_v, held_g, held_m, held_v, sem):
-    parts = [
-        (g.at[pl.ds(k * 38, 38)], held_g.at[pl.ds(k * 38, 38)], out_g.at[pl.ds(k * 38, 38)])
-        for k in range(5)
+    cuts = (0, 4, 8, 12, 16, 19)
+    groups = [pl.ds(a, b - a) for a, b in zip(cuts, cuts[1:])]
+    inward = [pltpu.make_async_copy(m, held_m, sem.at[0, 5])]
+    inward += [
+        pltpu.make_async_copy(g.at[at], held_g.at[at], sem.at[0, k])
+        for k, at in enumerate(groups)
     ]
-    parts.append((m, held_m, out_m))
-    parts.append((v, held_v, out_v))
-    inward = [pltpu.make_async_copy(p[0], p[1], sem.at[0, k]) for k, p in enumerate(parts)]
-    outward = [pltpu.make_async_copy(p[1], p[2], sem.at[1, k]) for k, p in enumerate(parts)]
+    inward.append(pltpu.make_async_copy(v, held_v, sem.at[0, 6]))
     for one in inward:
         one.start()
-    for one, other in zip(inward, outward):
-        one.wait()
-        other.start()
+    inward[0].wait()
+    outward = [pltpu.make_async_copy(held_m.at[0:10], out_m, sem.at[1, 5])]
+    outward[0].start()
+    gas = held_m[10:20] == 0.0
+    density = held_m[20:30]
+    for k, (a, b) in enumerate(zip(cuts, cuts[1:])):
+        inward[k + 1].wait()
+        for q in range(a, b):
+            held_g[q] = jnp.where(gas, density, held_g[q])
+        outward.append(
+            pltpu.make_async_copy(held_g.at[groups[k]], out_g.at[groups[k]], sem.at[1, k])
+        )
+        outward[-1].start()
+    inward[-1].wait()
+    outward.append(pltpu.make_async_copy(held_v, out_v, sem.at[1, 6]))
+    outward[-1].start()
     for one in outward:
         one.wait()
 
@@ -704,12 +707,12 @@
         g, m, v = pl.pallas_call(
             functools.partial(kernel, (nx, nz, ny)),
             out_shape=(
-                jax.ShapeDtypeStruct((190, 8, 128), F32),
-                jax.ShapeDtypeStruct((10, 8, 128), F32),
+                jax.ShapeDtypeStruct((19, 10, 8, 128), F32),
+                jax.ShapeDtypeStruct((30, 8, 128), F32),
                 jax.ShapeDtypeStruct((1, BUBBLES), F32),
             ),
             in_specs=[hbm] * 6,
-            out_specs=(vmem, vmem, vmem),
+            out_specs=(hbm, vmem, vmem),
             scratch_shapes=[
                 tiles(chips * (per_a + per_b) + 1),
                 tiles(20, jnp.int32),
@@ -726,14 +729,12 @@
                 pltpu.VMEM((19, 10, 8, 128), F32),
                 pltpu.VMEM((3, 10, 8, 128), F32),
                 tiles(10, jnp.int32),
-                tiles(10, jnp.int32),
                 tiles(10),
                 tiles(10),
                 tiles(10),
                 tiles(10),
                 tiles(10),
                 tiles(10),
-                tiles(BUBBLES),
                 pltpu.VMEM((ITERS, 2, 40, 128), F32),
                 pltpu.VMEM((ITERS, 2, 3, 40, 128), F32),
                 pltpu.VMEM((2, 56, 128), F32),
@@ -763,15 +764,15 @@
         g, m, v = pl.pallas_call(
             hand_over,
             out_shape=(
-                jax.ShapeDtypeStruct((190, 8, 128), F32),
+                jax.ShapeDtypeStruct((19, 10, 8, 128), F32),
                 jax.ShapeDtypeStruct((10, 8, 128), F32),
                 jax.ShapeDtypeStruct((1, BUBBLES), F32),
             ),
             in_specs=[anywhere] * 3,
             out_specs=(hbm, hbm, hbm),
             scratch_shapes=[
-                tiles(190),
-                tiles(10),
+                pltpu.VMEM((19, 10, 8, 128), F32),
+                tiles(30),
                 pltpu.VMEM((1, BUBBLES), F32),
                 pltpu.SemaphoreType.DMA((2, 7)),
             ],

time: 94.9 us -> 93.8 us (0.988)
  Pallas kernels: 94.2 us -> 93 us
    pallas_call x1, Pallas kernels: 92.1 us -> 90.9 us  [per_device(): pl.pallas_call(functools.partial(kernel, (nx, nz, ny)), out_shape=(jax.Sh...]
where the time goes in v4:
time: 93.8 us; the launch traced here: 93.6 us
  Pallas kernels  93 us (99%)
    pallas_call x1, Pallas kernels, per_device(): pl.pallas_call(functools.partial(kernel, (nx, nz, ny)), out_shape=(jax.Sh...  90.9 us
    pallas_call x1, Pallas kernels, per_device(): pl.pallas_call(hand_over, out_shape=(jax.ShapeDtypeStruct((19, 10, 8, 128...  2.05 us

profile of v4, /device:TPU:1, one launch (start us, length us, event | category | flops | bytes accessed | tf_op | source)
XLA Modules:
  0.0 93.6 jit_solution(16331228914206827081)
XLA Ops:
  0.6 90.9 %shard_map.85 = (f32[19,10,8,128]{3,2,1,0:T(8,128)}, f32[30,8,128]{2,1,0:T(8,128)}, f32[1,64]{1,0:T(1,128)}) custom-call(f32[190,8,128]{2,1,0:T(8,128)} %bitcast.7, f32[10,8,128]{2,1,0:T(8,128)} %bitcast.8, s32[10,8,128]{2,1,0:T(8,128)} %bitcast.9, s32[10,8,128]{2,1,0:T(8,128)} %bitcast.10, s32[64]{0:T(128)} %source_in.1, f32[64]{0:T(128)} %density_in.1), custom_call_target="tpu_custom_call" | custom-call | tf_op jit(solution)/shard_map/pallas_call | solution.py:707
  91.6 2.1 %shard_map.86 = (f32[19,10,8,128]{3,2,1,0:T(8,128)}, f32[10,8,128]{2,1,0:T(8,128)}, f32[1,64]{1,0:T(1,128)}) custom-call(f32[19,10,8,128]{3,2,1,0:T(8,128)} %get-tuple-element.9.g, f32[30,8,128]{2,1,0:T(8,128)} %get-tuple-element.10.m, f32[1,64]{1,0:T(1,128)} %get-tuple-element.11.v), custom_call_target="tpu_custom_call" | custom-call | tf_op jit(solution)/shard_map/pallas_call | solution.py:764

commit v5 on v4

--- a/solution.py
+++ b/solution.py
@@ -599,10 +599,10 @@
                 collide(step + 1, i, arrived(i))
                 return carry
 
+            middle_sum(step)
             lax.fori_loop(0, 10, again, 0)
             faces = send_faces(step + 1)
             started.append(faces)
-            middle_sum(step)
             post_columns(step + 1)
             wait_columns(cols_in.at[step + 1], cols, y_sem(step + 1, 0))
             for face in faces:
@@ -615,8 +615,8 @@
                     waiting[q, i] = value
                 return carry
 
+            middle_sum(step)
             lax.fori_loop(0, 10, last, 0)
-            middle_sum(step)
             store_g = pltpu.make_async_copy(waiting, out_g, fetch.at[0])
             store_g.start()
         total = end_sum(step)

time: 93.8 us -> 91.5 us (0.975)
  Pallas kernels: 93 us -> 90.7 us
    pallas_call x1, Pallas kernels: 90.9 us -> 88.7 us  [per_device(): pl.pallas_call(functools.partial(kernel, (nx, nz, ny)), out_shape=(jax.Sh...]
where the time goes in v5:
time: 91.5 us; the launch traced here: 91.4 us
  Pallas kernels  90.7 us (99%)
    pallas_call x1, Pallas kernels, per_device(): pl.pallas_call(functools.partial(kernel, (nx, nz, ny)), out_shape=(jax.Sh...  88.7 us
    pallas_call x1, Pallas kernels, per_device(): pl.pallas_call(hand_over, out_shape=(jax.ShapeDtypeStruct((19, 10, 8, 128...  2.05 us

profile of v5, /device:TPU:1, one launch (start us, length us, event | category | flops | bytes accessed | tf_op | source)
XLA Modules:
  0.0 91.4 jit_solution(13082929611931555943)
XLA Ops:
  0.6 88.7 %shard_map.85 = (f32[19,10,8,128]{3,2,1,0:T(8,128)}, f32[30,8,128]{2,1,0:T(8,128)}, f32[1,64]{1,0:T(1,128)}) custom-call(f32[190,8,128]{2,1,0:T(8,128)} %bitcast.7, f32[10,8,128]{2,1,0:T(8,128)} %bitcast.8, s32[10,8,128]{2,1,0:T(8,128)} %bitcast.9, s32[10,8,128]{2,1,0:T(8,128)} %bitcast.10, s32[64]{0:T(128)} %source_in.1, f32[64]{0:T(128)} %density_in.1), custom_call_target="tpu_custom_call" | custom-call | tf_op jit(solution)/shard_map/pallas_call | solution.py:707
  89.3 2.1 %shard_map.86 = (f32[19,10,8,128]{3,2,1,0:T(8,128)}, f32[10,8,128]{2,1,0:T(8,128)}, f32[1,64]{1,0:T(1,128)}) custom-call(f32[19,10,8,128]{3,2,1,0:T(8,128)} %get-tuple-element.9.g, f32[30,8,128]{2,1,0:T(8,128)} %get-tuple-element.10.m, f32[1,64]{1,0:T(1,128)} %get-tuple-element.11.v), custom_call_target="tpu_custom_call" | custom-call | tf_op jit(solution)/shard_map/pallas_call | solution.py:764

commit v6 on v5

--- a/solution.py
+++ b/solution.py
@@ -550,14 +550,14 @@
     lookup(table)
 
     gathered(1)
-    lax.fori_loop(0, 10, first, 0)
+    lax.fori_loop(0, 10, first, 0, unroll=5)
+    post_columns(0)
     faces = send_faces(0)
-    post_columns(0)
     started = [faces]
     kinds_right.wait_recv()
     kinds_left.wait_recv()
     wait_columns(kind_cols_in, kind_cols, KINDS + 2)
-    lax.fori_loop(0, 10, find_near, 0)
+    lax.fori_loop(0, 10, find_near, 0, unroll=5)
     volume_start = member_sums()
     wait_columns(cols_in.at[0], cols, y_sem(0, 0))
     for face in faces:
@@ -601,9 +601,9 @@
 
             middle_sum(step)
             lax.fori_loop(0, 10, again, 0)
+            post_columns(step + 1)
             faces = send_faces(step + 1)
             started.append(faces)
-            post_columns(step + 1)
             wait_columns(cols_in.at[step + 1], cols, y_sem(step + 1, 0))
             for face in faces:
                 face.wait_recv()

time: 91.5 us -> 90 us (0.984)
  Pallas kernels: 90.7 us -> 89.2 us
    pallas_call x1, Pallas kernels: 88.7 us -> 87.2 us  [per_device(): pl.pallas_call(functools.partial(kernel, (nx, nz, ny)), out_shape=(jax.Sh...]
where the time goes in v6:
time: 90 us; the launch traced here: 89.9 us
  Pallas kernels  89.2 us (99%)
    pallas_call x1, Pallas kernels, per_device(): pl.pallas_call(functools.partial(kernel, (nx, nz, ny)), out_shape=(jax.Sh...  87.2 us
    pallas_call x1, Pallas kernels, per_device(): pl.pallas_call(hand_over, out_shape=(jax.ShapeDtypeStruct((19, 10, 8, 128...  2.05 us

profile of v6, /device:TPU:1, one launch (start us, length us, event | category | flops | bytes accessed | tf_op | source)
XLA Modules:
  0.0 89.9 jit_solution(13210013907197326502)
XLA Ops:
  0.6 87.2 %shard_map.85 = (f32[19,10,8,128]{3,2,1,0:T(8,128)}, f32[30,8,128]{2,1,0:T(8,128)}, f32[1,64]{1,0:T(1,128)}) custom-call(f32[190,8,128]{2,1,0:T(8,128)} %bitcast.7, f32[10,8,128]{2,1,0:T(8,128)} %bitcast.8, s32[10,8,128]{2,1,0:T(8,128)} %bitcast.9, s32[10,8,128]{2,1,0:T(8,128)} %bitcast.10, s32[64]{0:T(128)} %source_in.1, f32[64]{0:T(128)} %density_in.1), custom_call_target="tpu_custom_call" | custom-call | tf_op jit(solution)/shard_map/pallas_call | solution.py:707
  87.8 2.1 %shard_map.86 = (f32[19,10,8,128]{3,2,1,0:T(8,128)}, f32[10,8,128]{2,1,0:T(8,128)}, f32[1,64]{1,0:T(1,128)}) custom-call(f32[19,10,8,128]{3,2,1,0:T(8,128)} %get-tuple-element.9.g, f32[30,8,128]{2,1,0:T(8,128)} %get-tuple-element.10.m, f32[1,64]{1,0:T(1,128)} %get-tuple-element.11.v), custom_call_target="tpu_custom_call" | custom-call | tf_op jit(solution)/shard_map/pallas_call | solution.py:764

commit v7 on v6

--- a/solution.py
+++ b/solution.py
@@ -600,7 +600,7 @@
                 return carry
 
             middle_sum(step)
-            lax.fori_loop(0, 10, again, 0)
+            lax.fori_loop(0, 10, again, 0, unroll=5)
             post_columns(step + 1)
             faces = send_faces(step + 1)
             started.append(faces)

time: 90 us -> 89.9 us (level)
  no operation moved by 1% of the time
where the time goes in v7:
time: 89.9 us; the launch traced here: 89.8 us
  Pallas kernels  89.1 us (99%)
    pallas_call x1, Pallas kernels, per_device(): pl.pallas_call(functools.partial(kernel, (nx, nz, ny)), out_shape=(jax.Sh...  87.1 us
    pallas_call x1, Pallas kernels, per_device(): pl.pallas_call(hand_over, out_shape=(jax.ShapeDtypeStruct((19, 10, 8, 128...  2.05 us

profile of v7, /device:TPU:1, one launch (start us, length us, event | category | flops | bytes accessed | tf_op | source)
XLA Modules:
  0.0 89.8 jit_solution(7656404843201598124)
XLA Ops:
  0.6 87.1 %shard_map.85 = (f32[19,10,8,128]{3,2,1,0:T(8,128)}, f32[30,8,128]{2,1,0:T(8,128)}, f32[1,64]{1,0:T(1,128)}) custom-call(f32[190,8,128]{2,1,0:T(8,128)} %bitcast.7, f32[10,8,128]{2,1,0:T(8,128)} %bitcast.8, s32[10,8,128]{2,1,0:T(8,128)} %bitcast.9, s32[10,8,128]{2,1,0:T(8,128)} %bitcast.10, s32[64]{0:T(128)} %source_in.1, f32[64]{0:T(128)} %density_in.1), custom_call_target="tpu_custom_call" | custom-call | tf_op jit(solution)/shard_map/pallas_call | solution.py:707
  87.7 2.1 %shard_map.86 = (f32[19,10,8,128]{3,2,1,0:T(8,128)}, f32[10,8,128]{2,1,0:T(8,128)}, f32[1,64]{1,0:T(1,128)}) custom-call(f32[19,10,8,128]{3,2,1,0:T(8,128)} %get-tuple-element.9.g, f32[30,8,128]{2,1,0:T(8,128)} %get-tuple-element.10.m, f32[1,64]{1,0:T(1,128)} %get-tuple-element.11.v), custom_call_target="tpu_custom_call" | custom-call | tf_op jit(solution)/shard_map/pallas_call | solution.py:764
